TPU v7x, 256 devices: a whole 4x4x8 slice. The times are simulated.
256 devices in a mesh: dp: 8 (over z_lo, core), slab: 32 (over z_hi, x, y).
Axes of the slice: x: 4, y: 4, z: 8 (z_hi: 2, z_lo: 4; z = z_hi * 4 + z_lo), core: 2. Of those that a mesh axis runs over, the one named last changes fastest.
Arguments:
- inputs: float32 [8, 16, 128, 128, 128], P('dp', None, 'slab'), may hold values from -6 to 6
- cotangent: float32 [8, 16, 128, 128, 128], P('dp', None, 'slab'), may hold values from -6 to 6
- spectral_weights: float32 [16, 16, 2, 12288], P(None, None, None, 'slab'), may hold values from -6 to 6
- pointwise_weights: float32 [16, 16], replicated, may hold values from -1.5 to 1.5
Outputs:
- grad_inputs: float32 [8, 16, 128, 128, 128], P('dp', None, 'slab')
- grad_spectral: float32 [16, 16, 2, 12288], P('dp', None, None, 'slab')
- grad_pointwise: float32 [16, 16], replicated
All inputs are finite; a program needn't handle non-finite values.
Results may differ from a plain program's by a relative error of at most 0.00011.
Values sent between devices are 32-bit elements; how exact they have to be, the bound alone decides.
A program may use at most 128 MiB of HBM per device.

v0:
```python
from functools import partial
import math

import jax
import jax.numpy as jnp
from jax import lax
from jax.sharding import PartitionSpec as P

NY = 128
NZ = 128
KX = 32
KY = 32
KZ = 12
XP = 4


def contract(pattern, left_operand, right_operand):
    return jnp.einsum(pattern, left_operand, right_operand, precision=lax.Precision.HIGHEST)


def twiddle(length, number, centered):
    places = lax.iota(jnp.int32, length)[:, None]
    orders = lax.iota(jnp.int32, number)[None, :]
    if centered:
        orders = jnp.where(orders < number // 2, orders, orders - number)
    angles = jnp.mod(places * orders, length).astype(jnp.float32) * (2.0 * math.pi / length)
    return (jnp.cos(angles), jnp.sin(angles))


def depth_weights():
    orders = lax.iota(jnp.int32, KZ)
    return jnp.where(orders == 0, 1.0, 2.0).astype(jnp.float32)


def forward_block(cosine, sine):
    top_row = jnp.stack([cosine, -sine], axis=1)
    low_row = jnp.stack([sine, cosine], axis=1)
    return jnp.stack([top_row, low_row], axis=1)


def inverse_block(cosine, sine):
    top_row = jnp.stack([cosine.T, sine.T], axis=1)
    low_row = jnp.stack([-sine.T, cosine.T], axis=1)
    return jnp.stack([top_row, low_row], axis=1)


def analyse_local(values, depth_table, second_table):
    partial_stack = contract("cxyz,zk->cxyk", values, depth_table)
    partial_stack = partial_stack.reshape(values.shape[0], values.shape[1], values.shape[2], 2, KZ)
    middle = contract("cxypk,ypsj->scxjk", partial_stack, second_table)
    return middle.reshape(2, values.shape[0], values.shape[1], KY * KZ)


def analyse_rows(received, first_table, norm_scale):
    final = contract("pcxq,xpsi->scqi", received, first_table) * norm_scale
    return final.reshape(2, received.shape[1], received.shape[3] * KX)


def synthesise_rows(stacked, first_inverse):
    spectra = stacked.reshape(2, stacked.shape[1], stacked.shape[2] // KX, KX)
    return contract("pcqi,ipsx->scxq", spectra, first_inverse)


def synthesise_local(received, second_inverse, depth_inverse, norm_scale):
    upper = received.reshape(2, received.shape[1], received.shape[2], KY, KZ)
    lower = contract("pcxjk,jpsy->scxyk", upper, second_inverse)
    result = contract("scxyk,skz->cxyz", lower, depth_inverse)
    return result * norm_scale


def body(inputs, cotangent, spectral_weights, pointwise_weights):
    values = inputs[0]
    upstream = cotangent[0]
    slab_count = lax.axis_size("slab")
    dp_count = lax.axis_size("dp")
    full_length = XP * slab_count
    norm_scale = 1.0 / math.sqrt(full_length * NY * NZ)
    third_cosine, third_sine = twiddle(NZ, KZ, False)
    second_cosine, second_sine = twiddle(NY, KY, True)
    first_cosine, first_sine = twiddle(full_length, KX, True)
    depth_scale = depth_weights()[None, :]
    plain_depth = jnp.concatenate([third_cosine, -third_sine], axis=1)
    weighted_depth = jnp.concatenate(
        [third_cosine * depth_scale, -third_sine * depth_scale], axis=1
    )
    plain_depth_inverse = jnp.stack([third_cosine.T, -third_sine.T])
    weighted_depth_inverse = jnp.stack(
        [(third_cosine * depth_scale).T, -(third_sine * depth_scale).T]
    )
    second_table = forward_block(second_cosine, second_sine)
    second_inverse = inverse_block(second_cosine, second_sine)
    first_table = forward_block(first_cosine, first_sine)
    first_inverse = inverse_block(first_cosine, first_sine)
    finish_rows = partial(analyse_rows, first_table=first_table, norm_scale=norm_scale)
    forward_stack = analyse_local(values, plain_depth, second_table)
    value_modes = finish_rows(
        lax.all_to_all(forward_stack, "slab", split_axis=3, concat_axis=2, tiled=True)
    )
    weight_real = spectral_weights[:, :, 0]
    weight_imag = spectral_weights[:, :, 1]
    mixed_real = contract("com,cm->om", weight_real, value_modes[0]) - contract(
        "com,cm->om", weight_imag, value_modes[1]
    )
    mixed_imag = contract("com,cm->om", weight_real, value_modes[1]) + contract(
        "com,cm->om", weight_imag, value_modes[0]
    )
    mixed_stack = synthesise_rows(jnp.stack([mixed_real, mixed_imag]), first_inverse)
    weighted_finish = partial(
        synthesise_local,
        second_inverse=second_inverse,
        depth_inverse=weighted_depth_inverse,
        norm_scale=norm_scale,
    )
    carried = weighted_finish(
        lax.all_to_all(mixed_stack, "slab", split_axis=2, concat_axis=3, tiled=True)
    )
    before = contract("co,cxyz->oxyz", pointwise_weights, values) + carried
    gelu_slope = 0.5 * (1.0 + lax.erf(before * (1.0 / math.sqrt(2.0)))) + before * jnp.exp(
        -0.5 * before * before
    ) * (1.0 / math.sqrt(2.0 * math.pi))
    grad_before = upstream * gelu_slope
    backward_stack = analyse_local(grad_before, weighted_depth, second_table)
    gradient_modes = finish_rows(
        lax.all_to_all(backward_stack, "slab", split_axis=3, concat_axis=2, tiled=True)
    )
    back_real = contract("com,om->cm", weight_real, gradient_modes[0]) + contract(
        "com,om->cm", weight_imag, gradient_modes[1]
    )
    back_imag = contract("com,om->cm", weight_real, gradient_modes[1]) - contract(
        "com,om->cm", weight_imag, gradient_modes[0]
    )
    back_stack = synthesise_rows(jnp.stack([back_real, back_imag]), first_inverse)
    plain_finish = partial(
        synthesise_local,
        second_inverse=second_inverse,
        depth_inverse=plain_depth_inverse,
        norm_scale=norm_scale,
    )
    spectral_back = plain_finish(
        lax.all_to_all(back_stack, "slab", split_axis=2, concat_axis=3, tiled=True)
    )
    grad_values = contract("co,oxyz->cxyz", pointwise_weights, grad_before) + spectral_back
    pointwise_part = contract("cxyz,oxyz->co", values, grad_before)
    pointwise_total = lax.psum(pointwise_part, ("dp", "slab"))
    grad_pointwise = pointwise_total / math.sqrt(dp_count * full_length * NY * NZ)
    rows_real = value_modes[0]
    rows_imag = value_modes[1]
    grad_real = (
        rows_real[:, None, :] * gradient_modes[0][None]
        + rows_imag[:, None, :] * gradient_modes[1][None]
    )
    grad_imag = (
        rows_real[:, None, :] * gradient_modes[1][None]
        - rows_imag[:, None, :] * gradient_modes[0][None]
    )
    grad_spectral = lax.psum_scatter(
        jnp.stack([grad_real, grad_imag], axis=2), "dp", scatter_dimension=0, tiled=True
    )
    return (grad_values[None], grad_spectral, grad_pointwise)


def solution(mesh):
    placed = (
        P("dp", None, "slab", None, None),
        P("dp", None, "slab", None, None),
        P(None, None, None, "slab"),
        P(),
    )
    return jax.shard_map(
        body,
        mesh=mesh,
        in_specs=placed,
        out_specs=(P("dp", None, "slab", None, None), P("dp", None, None, "slab"), P()),
        check_vma=False,
    )
```

profile of v0, /device:TPU:1, one launch (start us, length us, event | category | flops | bytes accessed | tf_op | source)
XLA Modules:
  0.0 306.5 jit_solution(9970833069103172918)
XLA Ops:
  7.4 5.3 %convolution_bitcast_fusion.4 = f32[16,4,128,24]{2,3,1,0:T(8,128)S(1)} fusion(f32[128,12]{0,1:T(8,128)S(1)} %get-tuple-element.49, f32[128,12]{0,1:T(8,128)S(1)} %get-tuple-element.50, f32[1,16,4,128,128]{4,3,2,1,0:T(8,128)} %param.4), kind=kOutput, calls=%fused_computation.19 | convolution fusion | flops 301992960 | bytes 4993024 | tf_op jit(solution)/shard_map/cxyz,zk->cxyk/dot_general | solution.py:18
  17.0 14.7 %all-to-all-start = ((f32[32,1,1536]{2,1,0:T(1,128)}), f32[32,1,1536]{2,1,0:T(1,128)S(1)}, u32[]{:S(2)}, u32[]{:S(2)}) async-start(f32[32,1,1536]{2,1,0:T(1,128)} %reshape.500), calls=%async_computation | async-start | bytes 393216 | tf_op jit(solution)/shard_map/all_to_all | solution.py:97
  33.9 2.2 fusion.104
  36.1 7.3 %all-to-all-done = f32[32,1,1536]{2,1,0:T(1,128)S(1)} async-done(((f32[32,1,1536]{2,1,0:T(1,128)}), f32[32,1,1536]{2,1,0:T(1,128)S(1)}, u32[]{:S(2)}, u32[]{:S(2)}) %all-to-all-start) | async-done | bytes 196640 | tf_op jit(solution)/shard_map/all_to_all | solution.py:97
  45.0 2.3 reshape.501
  47.2 3.4 %copy.212 = f32[2,16,4,32,12]{4,3,1,2,0:T(8,128)S(1)} copy(f32[2,16,4,32,12]{1,2,0,4,3:T(4,128)} %bitcast.273) | data formatting | bytes 393216 | tf_op jit(solution)/shard_map/all_to_all | solution.py:97
  50.6 3.2 %copy.104 = f32[2,16,32,4,12]{1,3,2,4,0:T(4,128)} copy(f32[2,16,32,4,12]{4,2,1,3,0:T(8,128)S(1)} %bitcast.269) | data formatting | bytes 393216 | tf_op jit(solution)/shard_map/all_to_all | solution.py:97
  53.8 4.0 %fusion.13 = f32[2,16,12,32]{3,1,2,0:T(8,128)S(1)} fusion(f32[2,16,128,12,1]{1,2,3,0,4:T(8,128)} %bitcast.274, f32[128,1,2,32]{0,3,1,2:T(8,128)S(1)} %get-tuple-element.38, f32[128,1,2,32]{0,3,1,2:T(8,128)S(1)} %get-tuple-element.37), kind=kOutput, calls=%fused_computation.25 | convolution fusion | flops 37777408 | bytes 311296 | tf_op jit(solution)/shard_map/pcxq,xpsi->scqi/dot_general | solution.py:18
  60.2 2.8 reshape.502
  63.0 4.9 %all-to-all-start.1 = ((f32[32,1,1536]{2,1,0:T(1,128)}), f32[32,1,1536]{2,1,0:T(1,128)S(1)}, u32[]{:S(2)}, u32[]{:S(2)}) async-start(f32[32,1,1536]{2,1,0:T(1,128)} %reshape.502), calls=%async_computation.1 | async-start | bytes 393216 | tf_op jit(solution)/shard_map/all_to_all | solution.py:115
  67.9 9.3 %fusion.10 = f32[16,4,128,128]{3,0,2,1:T(8,128)} fusion(f32[16,4,128,128]{3,2,1,0:T(8,128)} %bitcast.267, f32[16,16]{1,0:T(8,128)S(1)} %copy-done), kind=kOutput, calls=%fused_computation.13 | convolution fusion | flops 201326592 | bytes 8389632 | tf_op jit(solution)/shard_map/co,cxyz->oxyz/dot_general | solution.py:18
  77.3 2.4 all-to-all-done.1
  80.6 2.1 reshape.503
  85.1 7.4 %copy.171 = f32[2,16,4,128,12]{1,4,0,3,2:T(8,128)} copy(f32[2,16,4,128,12]{3,4,0,2,1:T(8,128)S(1)} %convolution_bitcast_fusion.1) | data formatting | bytes 1572864 | tf_op jit(solution)/shard_map/pcxjk,jpsy->scxyk/transpose | solution.py:18
  92.6 18.0 %fusion.4 = f32[16,4,128,128]{3,0,2,1:T(8,128)S(1)} fusion(f32[1,16,4,128,128]{4,3,2,1,0:T(8,128)} %param.5, f32[16,4,128,128]{3,0,2,1:T(8,128)} %fusion.10, f32[2,16,4,128,12]{1,4,0,3,2:T(8,128)} %copy.171, f32[1,12,128]{2,1,0:T(8,128)S(1)} %copy-done.8, f32[1,12,128]{2,1,0:T(8,128)S(1)} %copy-done.7), kind=kOutput, calls=%fused_computation.5 | convolution fusion | flops 313527296 | bytes 13381632 | tf_op jit(solution)/shard_map/scxyk,skz->cxyz/dot_general | solution.py:18
  112.6 5.1 %fusion.63 = f32[16,4,128,24]{3,0,2,1:T(8,128)} fusion(f32[16,4,128,128]{3,0,2,1:T(8,128)S(1)} %fusion.4, f32[128,12]{0,1:T(8,128)S(1)} %copy-done.10, f32[128,12]{0,1:T(8,128)S(1)} %copy-done.9), kind=kOutput, calls=%fused_computation.106 | convolution fusion | flops 301992960 | bytes 4993024 | tf_op jit(solution)/shard_map/cxyz,zk->cxyk/dot_general | solution.py:18
  117.7 3.3 %copy.116 = f32[16,4,128,24]{2,0,3,1:T(8,128)S(1)} copy(f32[16,4,128,24]{3,0,2,1:T(8,128)} %fusion.63) | data formatting | bytes 1572864 | tf_op jit(solution)/shard_map/cxyz,zk->cxyk/dot_general | solution.py:18
  124.9 9.4 %all-to-all-start.2 = ((f32[32,1,1536]{2,1,0:T(1,128)}), f32[32,1,1536]{2,1,0:T(1,128)S(1)}, u32[]{:S(2)}, u32[]{:S(2)}) async-start(f32[32,1,1536]{2,1,0:T(1,128)} %reshape.504), calls=%async_computation.2 | async-start | bytes 393216 | tf_op jit(solution)/shard_map/all_to_all | solution.py:124
  134.4 10.2 %fusion.16 = f32[16,16]{0,1:T(8,128)S(1)} fusion(f32[16,4,128,128]{3,0,2,1:T(8,128)} %copy-done.1, f32[16,4,128,128]{3,2,1,0:T(8,128)} %bitcast.268), kind=kOutput, calls=%fused_computation.28 | convolution fusion | flops 201326592 | bytes 8389632 | tf_op jit(solution)/shard_map/cxyz,oxyz->co/dot_general | solution.py:18
  144.5 79.1 %psum.7 = f32[16,16]{0,1:T(8,128)S(1)} all-reduce(f32[16,16]{0,1:T(8,128)S(1)} %fusion.16), channel_id=1, replica_groups=mesh['dp'=8,'slab'=32] {'dp','slab'}, use_global_device_ids=true, to_apply=%region_1.2 | all-reduce | flops 256 | bytes 2048 | tf_op jit(solution)/shard_map/psum | solution.py:144
  225.4 2.3 reshape.505
  227.6 3.4 %copy.219 = f32[2,16,4,32,12]{4,3,1,2,0:T(8,128)S(1)} copy(f32[2,16,4,32,12]{1,2,0,4,3:T(4,128)} %bitcast.278) | data formatting | bytes 393216 | tf_op jit(solution)/shard_map/all_to_all | solution.py:124
  231.0 3.2 %copy.121 = f32[2,16,32,4,12]{1,3,2,4,0:T(4,128)} copy(f32[2,16,32,4,12]{4,2,1,3,0:T(8,128)S(1)} %bitcast.270) | data formatting | bytes 393216 | tf_op jit(solution)/shard_map/all_to_all | solution.py:124
  234.2 4.0 %fusion.15 = f32[2,16,12,32]{3,1,2,0:T(8,128)S(1)} fusion(f32[2,16,128,12,1]{1,2,3,0,4:T(8,128)} %bitcast.271, f32[128,1,2,32]{0,3,1,2:T(8,128)S(1)} %get-tuple-element.38, f32[128,1,2,32]{0,3,1,2:T(8,128)S(1)} %get-tuple-element.37), kind=kOutput, calls=%fused_computation.27 | convolution fusion | flops 37777408 | bytes 311296 | tf_op jit(solution)/shard_map/pcxq,xpsi->scqi/dot_general | solution.py:18
  241.7 2.8 reshape.506
  244.6 7.2 %all-to-all-start.3 = ((f32[32,1,1536]{2,1,0:T(1,128)}), f32[32,1,1536]{2,1,0:T(1,128)S(1)}, u32[]{:S(2)}, u32[]{:S(2)}) async-start(f32[32,1,1536]{2,1,0:T(1,128)} %reshape.506), calls=%async_computation.3 | async-start | bytes 393216 | tf_op jit(solution)/shard_map/all_to_all | solution.py:140
  251.7 7.9 %fusion.72 = f32[4,128,128,16]{2,3,1,0:T(8,128)} fusion(f32[16,4,128,128]{3,0,2,1:T(8,128)} %copy-done.1, f32[16,16]{1,0:T(8,128)S(1)} %copy-done), kind=kOutput, calls=%fused_computation.121 | convolution fusion | flops 201326592 | bytes 8389632 | tf_op jit(solution)/shard_map/co,oxyz->cxyz/dot_general | solution.py:18
  259.6 5.5 %all-to-all-done.3 = f32[32,1,1536]{2,1,0:T(1,128)S(1)} async-done(((f32[32,1,1536]{2,1,0:T(1,128)}), f32[32,1,1536]{2,1,0:T(1,128)S(1)}, u32[]{:S(2)}, u32[]{:S(2)}) %all-to-all-start.3) | async-done | bytes 196640 | tf_op jit(solution)/shard_map/all_to_all | solution.py:140
  266.1 2.1 reshape.507
  270.5 7.4 %copy.206 = f32[2,16,4,128,12]{1,4,0,3,2:T(8,128)} copy(f32[2,16,4,128,12]{3,4,0,2,1:T(8,128)S(1)} %convolution_bitcast_fusion) | data formatting | bytes 1572864 | tf_op jit(solution)/shard_map/pcxjk,jpsy->scxyk/transpose | solution.py:18
  278.0 16.3 %fusion.6 = f32[1,16,4,128,128]{4,1,3,2,0:T(8,128)S(1)} fusion(f32[4,128,128,16]{2,3,1,0:T(8,128)} %fusion.72, f32[2,16,4,128,12]{1,4,0,3,2:T(8,128)} %copy.206, f32[1,12,128]{2,1,0:T(8,128)S(1)} %copy-done.6, f32[1,12,128]{2,1,0:T(8,128)S(1)} %get-tuple-element.51), kind=kOutput, calls=%fused_computation.8 | convolution fusion | flops 304090112 | bytes 9187328 | tf_op jit(solution)/shard_map/scxyk,skz->cxyz/dot_general | solution.py:18
  294.3 3.3 %copy.132 = f32[1,16,4,128,128]{4,3,2,1,0:T(8,128)} copy(f32[1,16,4,128,128]{4,1,3,2,0:T(8,128)S(1)} %fusion.6) | data formatting | bytes 8388608
  (85 shorter events, 29.8 us)
Async XLA Ops:
  7.2 60.8 %copy-start = (f32[16,16]{1,0:T(8,128)S(1)}, f32[16,16]{1,0:T(8,128)}, u32[]{:S(2)}) copy-start(f32[16,16]{1,0:T(8,128)} %param.7) | copy-start | bytes 3076
  17.0 26.4 %all-to-all-start = ((f32[32,1,1536]{2,1,0:T(1,128)}), f32[32,1,1536]{2,1,0:T(1,128)S(1)}, u32[]{:S(2)}, u32[]{:S(2)}) async-start(f32[32,1,1536]{2,1,0:T(1,128)} %reshape.500), calls=%async_computation | async-start | bytes 393216 | tf_op jit(solution)/shard_map/all_to_all | solution.py:97
  58.0 0.6 copy-start.2
  58.1 0.6 copy-start.4
  63.0 16.6 %all-to-all-start.1 = ((f32[32,1,1536]{2,1,0:T(1,128)}), f32[32,1,1536]{2,1,0:T(1,128)S(1)}, u32[]{:S(2)}, u32[]{:S(2)}) async-start(f32[32,1,1536]{2,1,0:T(1,128)} %reshape.502), calls=%async_computation.1 | async-start | bytes 393216 | tf_op jit(solution)/shard_map/all_to_all | solution.py:115
  85.1 7.5 %copy-start.7 = (f32[1,12,128]{2,1,0:T(8,128)S(1)}, f32[1,12,128]{2,1,0:T(8,128)}, u32[]{:S(2)}) copy-start(f32[1,12,128]{2,1,0:T(8,128)} %get-tuple-element.41) | copy-start | bytes 18436
  85.1 7.5 %copy-start.8 = (f32[1,12,128]{2,1,0:T(8,128)S(1)}, f32[1,12,128]{2,1,0:T(8,128)}, u32[]{:S(2)}) copy-start(f32[1,12,128]{2,1,0:T(8,128)} %get-tuple-element.42) | copy-start | bytes 18436
  92.6 20.1 %copy-start.9 = (f32[128,12]{0,1:T(8,128)S(1)}, f32[128,12]{0,1:T(8,128)}, u32[]{:S(2)}) copy-start(f32[128,12]{0,1:T(8,128)} %get-tuple-element.39) | copy-start | bytes 18436
  92.6 20.1 %copy-start.10 = (f32[128,12]{0,1:T(8,128)S(1)}, f32[128,12]{0,1:T(8,128)}, u32[]{:S(2)}) copy-start(f32[128,12]{0,1:T(8,128)} %get-tuple-element.40) | copy-start | bytes 18436
  110.6 2.0 copy-start.1
  124.9 99.4 %all-to-all-start.2 = ((f32[32,1,1536]{2,1,0:T(1,128)}), f32[32,1,1536]{2,1,0:T(1,128)S(1)}, u32[]{:S(2)}, u32[]{:S(2)}) async-start(f32[32,1,1536]{2,1,0:T(1,128)} %reshape.504), calls=%async_computation.2 | async-start | bytes 393216 | tf_op jit(solution)/shard_map/all_to_all | solution.py:124
  134.3 163.3 %reduce-scatter.2.cloned.1.call-start = ((), (), s32[]{:S(2)}) async-start(), calls=%async_computation.5 | async-start | bytes 884736 | tf_op jit(solution)/shard_map/reduce_scatter | solution.py:156
  231.0 7.5 %copy-start.3 = (f32[16,384]{1,0:T(8,128)S(1)}, f32[16,384]{1,0:T(8,128)}, u32[]{:S(2)}) copy-start(f32[16,384]{1,0:T(8,128)} %copy-done.2) | copy-start | bytes 73732
  231.0 7.5 %copy-start.5 = (f32[16,384]{1,0:T(8,128)S(1)}, f32[16,384]{1,0:T(8,128)}, u32[]{:S(2)}) copy-start(f32[16,384]{1,0:T(8,128)} %copy-done.4) | copy-start | bytes 73732
  244.6 20.5 %all-to-all-start.3 = ((f32[32,1,1536]{2,1,0:T(1,128)}), f32[32,1,1536]{2,1,0:T(1,128)S(1)}, u32[]{:S(2)}, u32[]{:S(2)}) async-start(f32[32,1,1536]{2,1,0:T(1,128)} %reshape.506), calls=%async_computation.3 | async-start | bytes 393216 | tf_op jit(solution)/shard_map/all_to_all | solution.py:140
  270.5 7.4 %copy-start.6 = (f32[1,12,128]{2,1,0:T(8,128)S(1)}, f32[1,12,128]{2,1,0:T(8,128)}, u32[]{:S(2)}) copy-start(f32[1,12,128]{2,1,0:T(8,128)} %get-tuple-element.52) | copy-start | bytes 18436
Sparse Core Ops, SparseCore 0:
  239.8 31.8 reduce-scatter.1
where the time goes:
time: 312 us; the launch traced here: 307 us
  matrix products  84.5 us (27%)
  blocking collectives  79.1 us (25%)
  local copies, waits for them, and re-layouts  68.5 us (22%)
  starting transfers between devices  36.2 us (12%)
  waiting for transfers between devices  15.2 us (5%)
  between operations  15.1 us (5%)
  other arithmetic  8.02 us (3%)
    dot_general x15, matrix products, contract(): jnp.einsum(pattern, left_operand, right_operand, precision=lax.Precision....  84.5 us
    psum x1, blocking collectives, body(): pointwise_total = lax.psum(pointwise_part, ('dp', 'slab'))  79.1 us
    unnamed x33, local copies, waits for them, and re-layouts  25.9 us
    transpose x4, local copies, waits for them, and re-layouts, contract(): jnp.einsum(pattern, left_operand, right_operand, precision=lax.Precision....  17.1 us
    all_to_all x1, starting transfers between devices, body(): lax.all_to_all(forward_stack, 'slab', split_axis=3, concat_axis=2, tiled=...  14.7 us
    all_to_all x1, starting transfers between devices, body(): lax.all_to_all(backward_stack, 'slab', split_axis=3, concat_axis=2, tiled...  9.43 us
    all_to_all x1, waiting for transfers between devices, body(): lax.all_to_all(forward_stack, 'slab', split_axis=3, concat_axis=2, tiled=...  7.33 us
    all_to_all x1, starting transfers between devices, body(): lax.all_to_all(back_stack, 'slab', split_axis=2, concat_axis=3, tiled=True)  7.16 us
  transfers between devices with their start and end apart: 5, of which 3 were waited for; matrix products, arithmetic and copies ran while one was open for 23% of the time, Pallas kernels for 0%

commit v1 on v0

v1 whole, which is shorter than its diff:
```python
import functools
import math

import jax
import jax.numpy as jnp
import ml_dtypes
import numpy as np
from jax import lax
from jax.experimental import pallas as pl
from jax.experimental.pallas import tpu as pltpu
from jax.sharding import PartitionSpec as P

CH = 16
XP = 4
NX = 128
NY = 128
NZ = 128
KX = 32
KY = 32
KZ = 12
SLAB = 32
DP = 8
ROWS = 16
F32 = jnp.float32
BF16 = jnp.bfloat16
MESH = pl.DeviceIdType.MESH
NORM = 1.0 / math.sqrt(NX * NY * NZ)


def halves(table):
    table = np.asarray(table, np.float64)
    high = table.astype(ml_dtypes.bfloat16)
    low = (table - high.astype(np.float64)).astype(ml_dtypes.bfloat16)
    return high, low


def angles(length, orders):
    places = np.arange(length)[:, None]
    return ((places * orders[None, :]) % length) * (2.0 * math.pi / length)


@functools.cache
def tables():
    centred = np.arange(KY)
    centred = np.where(centred < KY // 2, centred, centred - KY)
    second = angles(NY, centred)
    third = angles(NZ, np.arange(KZ))
    first = angles(NX, centred)
    ty = np.concatenate([np.cos(second).T, -np.sin(second).T], axis=0)
    ty_high, ty_low = halves(ty)
    ty_stack = np.concatenate(
        [np.concatenate([ty_high, ty_high], axis=1), np.concatenate([ty_low, np.zeros_like(ty_low)], axis=1)], axis=0
    )
    ty_inverse = np.concatenate([ty_high.T, ty_high.T, ty_low.T], axis=1)
    depth = {}
    for name, weights in (("plain", np.ones(KZ)), ("weighted", np.where(np.arange(KZ) == 0, 1.0, 2.0))):
        cosine = (np.cos(third) * weights[None, :]).T
        sine = (np.sin(third) * weights[None, :]).T
        real_row = np.concatenate([cosine, sine], axis=1)
        imag_row = np.concatenate([-sine, cosine], axis=1)
        analysis = np.zeros((2 * ROWS, 2 * NZ))
        analysis[:KZ] = real_row
        analysis[ROWS : ROWS + KZ] = imag_row
        synthesis = np.zeros((2, 15 * ROWS, 2 * NZ))
        synthesis[0, 7 * ROWS : 7 * ROWS + KZ] = real_row
        synthesis[1, 7 * ROWS : 7 * ROWS + KZ] = imag_row
        depth[name] = (np.concatenate(halves(analysis), axis=0),) + halves(synthesis)
    place = first.reshape(SLAB, XP, KX)
    cosine = np.cos(place).transpose(1, 0, 2) * NORM
    sine = np.sin(place).transpose(1, 0, 2) * NORM
    rows = np.zeros((2, XP, 4, SLAB, 2, 4, KX))
    for group in range(4):
        rows[0, :, group, :, 0, group] = cosine
        rows[1, :, group, :, 0, group] = sine
        rows[0, :, group, :, 1, group] = -sine
        rows[1, :, group, :, 1, group] = cosine
    rows_high, rows_low = halves(rows.reshape(2 * XP * 4 * SLAB, 2 * 4 * KX))
    return (ty_stack, ty_inverse) + depth["plain"] + depth["weighted"] + (rows_high, rows_low)


def split(value):
    high = value.astype(BF16)
    low = (value - high.astype(F32)).astype(BF16)
    return high, low


def dot(left, right):
    return jnp.dot(left, right, preferred_element_type=F32)


def dot_t(left, right):
    return lax.dot_general(left, right, (((1,), (1,)), ((), ())), preferred_element_type=F32)


def cat(pieces, axis):
    return jnp.concatenate(pieces, axis=axis)


def analyse_y(pair, ty_stack, store, group):
    high, low = split(pair)
    out = dot(ty_stack[...], cat([high, low], 0))
    out = out[:64] + out[64:]
    store[pl.ds(pl.multiple_of(group * 64, 64), 64), :] = out[:, :NZ]
    store[pl.ds(pl.multiple_of(group * 64 + 64, 64), 64), :] = out[:, NZ:]


def analyse_z(store, tz_stack, sbuf):
    lanes = lax.broadcasted_iota(jnp.int32, (ROWS, 128), 1) < 64

    def step(group, carry):
        pieces = []
        for each in range(4):
            j = group * 4 + each
            pieces.append(cat([store[pl.ds(j, 64, stride=64), :], store[pl.ds(KY + j, 64, stride=64), :]], 1))
        high, low = split(cat(pieces, 0))
        out = dot_t(tz_stack[...], high)
        out = out[:32] + out[32:] + dot_t(tz_stack[:32, :], low)
        for each in range(2):
            tile = out[:, 128 * each : 128 * each + 128]
            real, imag = tile[:ROWS], tile[ROWS:]
            first = jnp.where(lanes, real, pltpu.roll(imag, 64, axis=1))
            second = jnp.where(lanes, pltpu.roll(real, 64, axis=1), imag)
            base = pl.multiple_of((group * 4 + 2 * each) * ROWS, ROWS)
            sbuf[pl.ds(base, ROWS), :] = first
            sbuf[pl.ds(base + ROWS, ROWS), :] = second
        return carry

    lax.fori_loop(0, KY // 4, step, 0)


def analyse_x(rbuf, rows_high, rows_low):
    parts = []
    for t in range(3):
        block = cat([rbuf[pl.ds(4 * t + k, SLAB, stride=ROWS), :] for k in range(4)], 0).T
        parts.append(cat([block[16 * q : 16 * q + 16] for q in range(8)], 1))
    high, low = split(cat(parts, 0))
    out = dot(cat([high, low], 0), rows_high[...])
    return out[:48] + out[48:] + dot(high, rows_low[...])


def synthesise_x(modes, rows_high, rows_low, sbuf):
    high, low = split(modes)
    out = dot_t(cat([high, low], 0), rows_high[...])
    out = out[:48] + out[48:] + dot_t(high, rows_low[...])
    for t in range(3):
        part = out[16 * t : 16 * t + 16]
        block = cat([part[:, 128 * q : 128 * q + 128] for q in range(8)], 0).T
        for k in range(4):
            sbuf[pl.ds(4 * t + k, SLAB, stride=ROWS), :] = block[SLAB * k : SLAB * k + SLAB]


def synthesise_z(rbuf, zi_high, zi_low, held, store):
    for g in range(4):
        block = rbuf[pl.ds(128 * g, 128), :].T
        high, low = split(cat([block[:64], block[64:]], 1))
        held[pl.ds(64 * g, 64), :] = high
        held[pl.ds(256 + 64 * g, 64), :] = low

    def step(jj, carry):
        at = pl.multiple_of(7 * ROWS - ROWS * jj, ROWS)
        table_high = cat([zi_high[0, pl.ds(at, 128), :], zi_high[1, pl.ds(at, 128), :]], 0)
        table_low = cat([zi_low[0, pl.ds(at, 128), :], zi_low[1, pl.ds(at, 128), :]], 0)
        out = dot(held[...], table_high)
        out = out[:256] + out[256:] + dot(held[:256, :], table_low)
        for g in range(4):
            store[pl.ds(8 * g + jj, 64, stride=64), :] = out[64 * g : 64 * g + 64, :NZ]
            store[pl.ds(KY + 8 * g + jj, 64, stride=64), :] = out[64 * g : 64 * g + 64, NZ:]
        return carry

    lax.fori_loop(0, 8, step, 0)


def synthesise_y(store, ty_inverse, group):
    pair = cat(
        [
            store[pl.ds(pl.multiple_of(group * 64, 64), 64), :],
            store[pl.ds(pl.multiple_of(group * 64 + 64, 64), 64), :],
        ],
        1,
    )
    high, low = split(pair)
    return dot(ty_inverse[...], cat([high, low, high], 0))


def rows_of(source, x, y0):
    left = cat([source[c, x, pl.ds(y0, 8), :] for c in range(CH)], 0)
    right = cat([source[c, x, pl.ds(y0 + 8, 8), :] for c in range(CH)], 0)
    return cat([left, right], 1)


def mix_channels(kron, halves_stack, target, x, y0):
    out = dot(kron[...], halves_stack)
    out = out[:128] + out[128:]
    for c in range(CH):
        target[c, x, pl.ds(y0, 8), :] = out[8 * c : 8 * c + 8, :NZ]
        target[c, x, pl.ds(y0 + 8, 8), :] = out[8 * c : 8 * c + 8, NZ:]


def kernel(
    x_hbm, cot_hbm, w_hbm, pw_ref, ty_stack, ty_inverse, tz_plain, zp_high, zp_low, tz_weighted, zw_high, zw_low,
    rows_high, rows_low,
    gi_hbm, gs_ref, gp_ref,
    xv, cv, bv, wv, store, store2, held, sbuf, rbuf, vv, gv, kron1, kron2, pacc,
    vsend, vrecv, gsend, grecv, psend, precv,
    xsem, csem, wsem, osem, ssem, rsem, vssem, vrsem, gssem, grsem, pssem, prsem,
):
    me = lax.axis_index("slab")
    mine = lax.axis_index("dp")

    barrier = pltpu.get_barrier_semaphore()

    def greet_slab(d, carry):
        pl.semaphore_signal(barrier, inc=1, device_id={"slab": lax.rem(me + d, SLAB)}, device_id_type=MESH)
        return carry

    def greet_dp(d, carry):
        pl.semaphore_signal(barrier, inc=1, device_id={"dp": lax.rem(mine + d, DP)}, device_id_type=MESH)
        return carry

    def x_copy(c):
        return pltpu.make_async_copy(x_hbm.at[pl.ds(2 * c, 2)], xv.at[pl.ds(2 * c, 2)], xsem.at[c])

    for c in range(CH // 2):
        x_copy(c).start()
    w_copy = pltpu.make_async_copy(w_hbm, wv, wsem)
    w_copy.start()
    c_copy = pltpu.make_async_copy(cot_hbm, cv, csem)
    c_copy.start()
    lax.fori_loop(1, SLAB, greet_slab, 0)
    lax.fori_loop(1, DP, greet_dp, 0)

    def slab_copy(phase, p, slot):
        return pltpu.make_async_remote_copy(
            src_ref=sbuf.at[phase, pl.ds(pl.multiple_of(ROWS * p, ROWS), ROWS)],
            dst_ref=rbuf.at[phase, pl.ds(pl.multiple_of(ROWS * slot, ROWS), ROWS)],
            send_sem=ssem.at[phase, p],
            recv_sem=rsem.at[phase, slot],
            device_id={"slab": p},
            device_id_type=MESH,
        )

    def send_all(phase):
        def step(d, carry):
            slab_copy(phase, lax.rem(me + d, SLAB), me).start()
            return carry

        lax.fori_loop(1, SLAB, step, 0)
        own = pl.ds(pl.multiple_of(ROWS * me, ROWS), ROWS)
        rbuf[phase, own, :] = sbuf[phase, own, :]

    def receive_all(phase):
        def step(d, carry):
            peer = lax.rem(me + d, SLAB)
            slab_copy(phase, peer, peer).wait_recv()
            return carry

        lax.fori_loop(1, SLAB, step, 0)

    def sent_all(phase):
        def step(d, carry):
            slab_copy(phase, lax.rem(me + d, SLAB), me).wait_send()
            return carry

        lax.fori_loop(1, SLAB, step, 0)

    spread = (
        lax.broadcasted_iota(jnp.int32, (128, CH), 0) // 8 == lax.broadcasted_iota(jnp.int32, (128, CH), 1)
    ).astype(F32)
    same_row = (
        lax.broadcasted_iota(jnp.int32, (128, 128), 0) % 8 == lax.broadcasted_iota(jnp.int32, (128, 128), 1) % 8
    )
    wide = jnp.dot(spread, pw_ref[...], precision=lax.Precision.HIGHEST, preferred_element_type=F32)
    wide = lax.dot_general(
        wide, spread, (((1,), (1,)), ((), ())), precision=lax.Precision.HIGHEST, preferred_element_type=F32
    )
    wide = jnp.where(same_row, wide, 0.0)
    for kron, value in ((kron1, wide.T), (kron2, wide)):
        high, low = split(value)
        kron[...] = cat([cat([high, high], 1), cat([low, jnp.zeros_like(low)], 1)], 0)
    for phase in (1, 3):
        for k in range(KZ, ROWS):
            sbuf[phase, pl.ds(k, SLAB, stride=ROWS), :] = jnp.zeros((SLAB, 128), F32)

    def forward_step(c, carry):
        x_copy(c).wait()
        for x in range(XP):
            analyse_y(cat([xv[2 * c, x], xv[2 * c + 1, x]], 1), ty_stack, store, x * CH + 2 * c)
        return carry

    lax.fori_loop(0, CH // 2, forward_step, 0)
    analyse_z(store, tz_plain, sbuf.at[0])
    pl.semaphore_wait(barrier, SLAB - 1 + DP - 1)
    send_all(0)

    def mix_step(yg, carry):
        y0 = pl.multiple_of(yg * 16, 16)
        for x in range(XP):
            high, low = split(rows_of(xv, x, y0))
            mix_channels(kron1, cat([high, low], 0), bv, x, y0)
        return carry

    lax.fori_loop(0, NY // 16, mix_step, 0)
    w_copy.wait()
    receive_all(0)
    modes = analyse_x(rbuf.at[0], rows_high, rows_low)
    vv[:48, :] = modes[:, :128]
    vv[48:, :] = modes[:, 128:]

    def mode_step(c, carry):
        out = []
        for t in range(3):
            wr = wv[c, :, 0, 128 * t : 128 * t + 128]
            wi = wv[c, :, 1, 128 * t : 128 * t + 128]
            vr = vv[pl.ds(16 * t + c, 1), :]
            vi = vv[pl.ds(48 + 16 * t + c, 1), :]
            out.append(carry[2 * t] + (wr * vr - wi * vi))
            out.append(carry[2 * t + 1] + (wr * vi + wi * vr))
        return tuple(out)

    mixed = lax.fori_loop(0, CH, mode_step, tuple(jnp.zeros((CH, 128), F32) for _ in range(6)))
    mixed = cat([cat([mixed[2 * t], mixed[2 * t + 1]], 1) for t in range(3)], 0)
    synthesise_x(mixed, rows_high, rows_low, sbuf.at[1])
    send_all(1)

    def v_copy(d, slot):
        return pltpu.make_async_remote_copy(
            src_ref=vsend.at[pl.ds(pl.multiple_of(16 * d, 16), 16)],
            dst_ref=vrecv.at[pl.ds(pl.multiple_of(16 * slot, 16), 16)],
            send_sem=vssem.at[d],
            recv_sem=vrsem.at[slot],
            device_id={"dp": d},
            device_id_type=MESH,
        )

    vsend[...] = jnp.zeros_like(vsend)
    for d in range(DP):
        for c in range(2):
            for t in range(3):
                row = 16 * t + 2 * d + c
                at = 16 * d + 6 * c + t
                vsend[at : at + 1, :] = vv[row : row + 1, :]
                vsend[at + 3 : at + 4, :] = vv[row + 48 : row + 49, :]

    def v_send(d, carry):
        v_copy(lax.rem(mine + d, DP), mine).start()
        return carry

    lax.fori_loop(1, DP, v_send, 0)
    own_v = pl.ds(pl.multiple_of(16 * mine, 16), 16)
    vrecv[own_v, :] = vsend[own_v, :]

    c_copy.wait()
    receive_all(1)

    synthesise_z(rbuf.at[1], zw_high, zw_low, held, store)

    def middle_step(o, carry):
        for x in range(XP):
            carried = synthesise_y(store, ty_inverse, x * CH + 2 * o)
            grads = []
            for each in range(2):
                before = carried[:, NZ * each : NZ * each + NZ] + bv[2 * o + each, x]
                slope = 0.5 * (1.0 + lax.erf(before * (1.0 / math.sqrt(2.0)))) + before * jnp.exp(
                    -0.5 * before * before
                ) * (1.0 / math.sqrt(2.0 * math.pi))
                grad = cv[2 * o + each, x] * slope
                cv[2 * o + each, x] = grad
                grads.append(grad)
            analyse_y(cat(grads, 1), ty_stack, store2, x * CH + 2 * o)
        return carry

    lax.fori_loop(0, CH // 2, middle_step, 0)
    analyse_z(store2, tz_weighted, sbuf.at[2])
    send_all(2)

    pacc[...] = jnp.zeros_like(pacc)

    def back_step(yg, carry):
        y0 = pl.multiple_of(yg * 16, 16)
        for x in range(XP):
            high, low = split(rows_of(cv, x, y0))
            stack = cat([high, low], 0)
            mix_channels(kron2, stack, bv, x, y0)
            xhigh, xlow = split(rows_of(xv, x, y0))
            pacc[...] += dot_t(cat([xhigh, xlow], 0), stack)
        return carry

    lax.fori_loop(0, NY // 16, back_step, 0)
    part = pacc[:128, :128] + pacc[:128, 128:] + pacc[128:, :128] + pacc[128:, 128:]
    part = jnp.where(same_row, part, 0.0)
    part = jnp.dot(part, spread, precision=lax.Precision.HIGHEST, preferred_element_type=F32)
    part = lax.dot_general(
        spread, part, (((0,), (0,)), ((), ())), precision=lax.Precision.HIGHEST, preferred_element_type=F32
    )
    gsend[96:112, :] = cat([part, jnp.zeros((CH, 128 - CH), F32)], 1)

    receive_all(2)
    modes = analyse_x(rbuf.at[2], rows_high, rows_low)
    gv[:48, :] = modes[:, :128]
    gv[48:, :] = modes[:, 128:]

    def back_mode_step(c, carry):
        for t in range(3):
            wr = wv[c, :, 0, 128 * t : 128 * t + 128]
            wi = wv[c, :, 1, 128 * t : 128 * t + 128]
            gr = gv[16 * t : 16 * t + 16, :]
            gi = gv[48 + 16 * t : 64 + 16 * t, :]
            vv[pl.ds(16 * t + c, 1), :] = jnp.sum(wr * gr + wi * gi, axis=0, keepdims=True)
            vv[pl.ds(48 + 16 * t + c, 1), :] = jnp.sum(wr * gi - wi * gr, axis=0, keepdims=True)
        return carry

    lax.fori_loop(0, CH, back_mode_step, 0)
    synthesise_x(cat([vv[:48, :], vv[48:, :]], 1), rows_high, rows_low, sbuf.at[3])
    send_all(3)

    def g_copy(d, slot):
        return pltpu.make_async_remote_copy(
            src_ref=gsend,
            dst_ref=grecv.at[pl.ds(pl.multiple_of(112 * slot, 16), 112)],
            send_sem=gssem.at[d],
            recv_sem=grsem.at[slot],
            device_id={"dp": d},
            device_id_type=MESH,
        )

    gsend[:96, :] = gv[...]

    def g_send(d, carry):
        g_copy(lax.rem(mine + d, DP), mine).start()
        return carry

    lax.fori_loop(1, DP, g_send, 0)
    grecv[pl.ds(pl.multiple_of(112 * mine, 16), 112), :] = gsend[...]

    def dp_receive(d, carry):
        peer = lax.rem(mine + d, DP)
        g_copy(peer, peer).wait_recv()
        v_copy(peer, peer).wait_recv()
        return carry

    lax.fori_loop(1, DP, dp_receive, 0)

    for c in range(2):
        def sample_step(d, carry):
            out = []
            base = pl.multiple_of(112 * d, 16)
            for t in range(3):
                vr = vrecv[pl.ds(16 * d + 6 * c + t, 1), :]
                vi = vrecv[pl.ds(16 * d + 6 * c + 3 + t, 1), :]
                gr = grecv[pl.ds(base + 16 * t, 16), :]
                gi = grecv[pl.ds(base + 48 + 16 * t, 16), :]
                out.append(carry[2 * t] + (gr * vr + gi * vi))
                out.append(carry[2 * t + 1] + (gi * vr - gr * vi))
            return tuple(out)

        total = lax.fori_loop(0, DP, sample_step, tuple(jnp.zeros((CH, 128), F32) for _ in range(6)))
        for t in range(3):
            gs_ref[c, :, 0, 128 * t : 128 * t + 128] = total[2 * t]
            gs_ref[c, :, 1, 128 * t : 128 * t + 128] = total[2 * t + 1]

    def p_copy(p, slot):
        return pltpu.make_async_remote_copy(
            src_ref=psend,
            dst_ref=precv.at[pl.ds(pl.multiple_of(16 * slot, 16), 16)],
            send_sem=pssem.at[p],
            recv_sem=prsem.at[slot],
            device_id={"slab": p},
            device_id_type=MESH,
        )

    psum = grecv[96:112, :]
    for d in range(1, DP):
        psum = psum + grecv[112 * d + 96 : 112 * d + 112, :]
    psend[...] = psum

    def p_send(d, carry):
        p_copy(lax.rem(me + d, SLAB), me).start()
        return carry

    lax.fori_loop(1, SLAB, p_send, 0)
    precv[pl.ds(pl.multiple_of(16 * me, 16), 16), :] = psum

    receive_all(3)

    synthesise_z(rbuf.at[3], zp_high, zp_low, held, store)

    def o_copy(c):
        return pltpu.make_async_copy(bv.at[pl.ds(2 * c, 2)], gi_hbm.at[pl.ds(2 * c, 2)], osem.at[c])

    def last_step(c, carry):
        for x in range(XP):
            out = synthesise_y(store, ty_inverse, x * CH + 2 * c)
            bv[2 * c, x] = bv[2 * c, x] + out[:, :NZ]
            bv[2 * c + 1, x] = bv[2 * c + 1, x] + out[:, NZ:]
        o_copy(c).start()
        return carry

    lax.fori_loop(0, CH // 2, last_step, 0)

    def p_receive(d, carry):
        peer = lax.rem(me + d, SLAB)
        p_copy(peer, peer).wait_recv()
        return carry

    lax.fori_loop(1, SLAB, p_receive, 0)
    total = precv[0:16, :]
    for s in range(1, SLAB):
        total = total + precv[16 * s : 16 * s + 16, :]
    gp_ref[...] = total[:, :CH] * (1.0 / math.sqrt(DP * NX * NY * NZ))

    for phase in range(4):
        sent_all(phase)

    def dp_sent(d, carry):
        peer = lax.rem(mine + d, DP)
        v_copy(peer, mine).wait_send()
        g_copy(peer, mine).wait_send()
        return carry

    lax.fori_loop(1, DP, dp_sent, 0)

    def p_sent(d, carry):
        p_copy(lax.rem(me + d, SLAB), me).wait_send()
        return carry

    lax.fori_loop(1, SLAB, p_sent, 0)
    for c in range(CH // 2):
        o_copy(c).wait()


def body(inputs, cotangent, spectral_weights, pointwise_weights):
    constants = [jnp.asarray(table) for table in tables()]
    anywhere = pl.BlockSpec(memory_space=pl.ANY)
    vmem = pl.BlockSpec(memory_space=pltpu.VMEM)
    block = (CH, XP, NY, NZ)
    dma = pltpu.SemaphoreType.DMA
    grad_inputs, grad_spectral, grad_pointwise = pl.pallas_call(
        kernel,
        out_shape=[
            jax.ShapeDtypeStruct(block, F32),
            jax.ShapeDtypeStruct((2, CH, 2, KX * KZ), F32),
            jax.ShapeDtypeStruct((CH, CH), F32),
        ],
        in_specs=[anywhere] * 3 + [vmem] * (1 + len(constants)),
        out_specs=[anywhere, vmem, vmem],
        scratch_shapes=[
            pltpu.VMEM(block, F32),
            pltpu.VMEM(block, F32),
            pltpu.VMEM(block, F32),
            pltpu.VMEM((CH, CH, 2, KX * KZ), F32),
            pltpu.VMEM((CH * XP * 64, NZ), F32),
            pltpu.VMEM((CH * XP * 64, NZ), F32),
            pltpu.VMEM((512, 256), BF16),
            pltpu.VMEM((4, SLAB * ROWS, 128), F32),
            pltpu.VMEM((4, SLAB * ROWS, 128), F32),
            pltpu.VMEM((96, 128), F32),
            pltpu.VMEM((96, 128), F32),
            pltpu.VMEM((256, 256), BF16),
            pltpu.VMEM((256, 256), BF16),
            pltpu.VMEM((256, 256), F32),
            pltpu.VMEM((16 * DP, 128), F32),
            pltpu.VMEM((16 * DP, 128), F32),
            pltpu.VMEM((112, 128), F32),
            pltpu.VMEM((112 * DP, 128), F32),
            pltpu.VMEM((16, 128), F32),
            pltpu.VMEM((16 * SLAB, 128), F32),
            dma((CH // 2,)),
            dma,
            dma,
            dma((CH // 2,)),
            dma((4, SLAB)),
            dma((4, SLAB)),
            dma((DP,)),
            dma((DP,)),
            dma((DP,)),
            dma((DP,)),
            dma((SLAB,)),
            dma((SLAB,)),
        ],
        compiler_params=pltpu.CompilerParams(
            collective_id=0, has_side_effects=True, vmem_limit_bytes=48 * 1024 * 1024
        ),
        name="layer_backward",
    )(inputs.reshape(block), cotangent.reshape(block), spectral_weights, pointwise_weights, *constants)
    return (grad_inputs[None], grad_spectral, grad_pointwise)


def solution(mesh):
    placed = (
        P("dp", None, "slab", None, None),
        P("dp", None, "slab", None, None),
        P(None, None, None, "slab"),
        P(),
    )
    return jax.shard_map(
        body,
        mesh=mesh,
        in_specs=placed,
        out_specs=(P("dp", None, "slab", None, None), P("dp", None, None, "slab"), P()),
        check_vma=False,
    )
```

time: 312 us -> 104 us (0.33)
  the two profiles are of different devices: /device:TPU:1 before, /device:TPU:99 now
where the time goes in v1:
time: 104 us
  Pallas kernels  86.3 us (83%)
  local copies, waits for them, and re-layouts  16.8 us (16%)
    pallas_call x1, Pallas kernels, body(): pl.pallas_call(kernel, out_shape=[jax.ShapeDtypeStruct(block, F32), jax.S...  86.3 us
    unnamed x27, local copies, waits for them, and re-layouts  16.8 us

profile of v1, /device:TPU:99, one launch (start us, length us, event | category | flops | bytes accessed | tf_op | source)
XLA Modules:
  0.0 103.8 jit_solution(4481458648531593365)
XLA Ops:
  0.6 0.0 copy-start
  0.6 1.1 %copy-done = f32[16,16,2,384]{3,2,1,0:T(2,128)S(1)} copy-done((f32[16,16,2,384]{3,2,1,0:T(2,128)S(1)}, f32[16,16,2,384]{3,2,1,0:T(2,128)}, u32[]{:S(2)}) %copy-start) | copy-done | bytes 786456
  1.8 0.0 copy-start.1
  1.8 1.0 %copy-done.1 = bf16[1024,256]{1,0:T(8,128)(2,1)S(1)} copy-done((bf16[1024,256]{1,0:T(8,128)(2,1)S(1)}, bf16[1024,256]{1,0:T(8,128)(2,1)}, u32[]{:S(2)}) %copy-start.1) | copy-done | bytes 524312
  2.8 0.0 copy-start.2
  2.8 1.0 %copy-done.2 = bf16[1024,256]{1,0:T(8,128)(2,1)S(1)} copy-done((bf16[1024,256]{1,0:T(8,128)(2,1)S(1)}, bf16[1024,256]{1,0:T(8,128)(2,1)}, u32[]{:S(2)}) %copy-start.2) | copy-done | bytes 524312
  3.8 0.0 copy-start.3
  3.9 0.9 copy-done.3
  4.8 0.0 copy-start.4
  4.8 0.9 copy-done.4
  5.7 0.0 copy-start.5
  5.7 0.9 copy-done.5
  6.7 0.0 copy-start.6
  6.7 0.9 copy-done.6
  7.6 0.0 copy-start.7
  7.6 0.8 copy-done.7
  8.5 0.0 copy-start.8
  8.5 0.8 copy-done.8
  9.3 0.0 copy-start.9
  9.3 0.8 copy-done.9
  10.1 0.0 copy-start.10
  10.1 0.8 copy-done.10
  10.8 0.0 copy-start.11
  10.8 0.7 copy-done.11
  11.5 86.3 %layer_backward.1 = (f32[16,4,128,128]{3,2,1,0:T(8,128)}, f32[2,16,2,384]{3,2,1,0:T(2,128)S(1)}, f32[16,16]{1,0:T(8,128)S(1)}) custom-call(f32[16,4,128,128]{3,2,1,0:T(8,128)} %bitcast.3, f32[16,4,128,128]{3,2,1,0:T(8,128)} %bitcast.4, f32[16,16,2,384]{3,2,1,0:T(2,128)S(1)} %copy-done, f32[16,16]{1,0:T(8,128)S(1)} %copy-done.11, ...), custom_call_target="tpu_custom_call" | custom-call | tf_op jit(solution)/shard_map/layer_backward/pallas_call | solution.py:537
  97.9 4.7 %copy.20 = f32[1,16,4,128,128]{4,3,2,1,0:T(8,128)} copy(f32[1,16,4,128,128]{4,3,2,1,0:T(8,128)} %bitcast.5) | data formatting | bytes 8388608
  102.6 0.6 copy.21
  103.2 0.6 copy.22
Async XLA Ops:
  0.6 1.1 %copy-start = (f32[16,16,2,384]{3,2,1,0:T(2,128)S(1)}, f32[16,16,2,384]{3,2,1,0:T(2,128)}, u32[]{:S(2)}) copy-start(f32[16,16,2,384]{3,2,1,0:T(2,128)} %w_hbm.1) | copy-start | bytes 2359300
  1.8 1.0 %copy-start.1 = (bf16[1024,256]{1,0:T(8,128)(2,1)S(1)}, bf16[1024,256]{1,0:T(8,128)(2,1)}, u32[]{:S(2)}) copy-start(bf16[1024,256]{1,0:T(8,128)(2,1)} %constant.29.clone.rows_low) | copy-start | bytes 1572868
  2.8 1.0 %copy-start.2 = (bf16[1024,256]{1,0:T(8,128)(2,1)S(1)}, bf16[1024,256]{1,0:T(8,128)(2,1)}, u32[]{:S(2)}) copy-start(bf16[1024,256]{1,0:T(8,128)(2,1)} %constant.28.clone.rows_high) | copy-start | bytes 1572868
  3.8 0.9 copy-start.3
  4.8 0.9 copy-start.4
  5.7 0.9 copy-start.5
  6.7 0.9 copy-start.6
  7.6 0.8 copy-start.7
  8.5 0.8 copy-start.8
  9.3 0.8 copy-start.9
  10.1 0.8 copy-start.10
  10.8 0.7 copy-start.11

commit v2 on v1

v2 whole, which is shorter than its diff:
```python
import functools
import math

import jax
import jax.numpy as jnp
import ml_dtypes
import numpy as np
from jax import lax
from jax.experimental import pallas as pl
from jax.experimental.pallas import tpu as pltpu
from jax.sharding import PartitionSpec as P

CH = 16
XP = 4
NX = 128
NY = 128
NZ = 128
KX = 32
KY = 32
KZ = 12
SLAB = 32
DP = 8
ROWS = 16
PITCH = 72
F32 = jnp.float32
BF16 = jnp.bfloat16
MESH = pl.DeviceIdType.MESH
NORM = 1.0 / math.sqrt(NX * NY * NZ)


def halves(table):
    table = np.asarray(table, np.float64)
    high = table.astype(ml_dtypes.bfloat16)
    low = (table - high.astype(np.float64)).astype(ml_dtypes.bfloat16)
    return high, low


def angles(length, orders):
    places = np.arange(length)[:, None]
    return ((places * orders[None, :]) % length) * (2.0 * math.pi / length)


@functools.cache
def tables():
    centred = np.arange(KY)
    centred = np.where(centred < KY // 2, centred, centred - KY)
    second = angles(NY, centred)
    third = angles(NZ, np.arange(KZ))
    first = angles(NX, centred)
    ty = np.concatenate([np.cos(second).T, -np.sin(second).T], axis=0)
    ty_high, ty_low = halves(ty)
    ty_stack = np.concatenate(
        [np.concatenate([ty_high, ty_high], axis=1), np.concatenate([ty_low, np.zeros_like(ty_low)], axis=1)], axis=0
    )
    ty_inverse = np.concatenate([ty_high.T, ty_high.T, ty_low.T], axis=1)
    depth = {}
    for name, weights in (("plain", np.ones(KZ)), ("weighted", np.where(np.arange(KZ) == 0, 1.0, 2.0))):
        cosine = (np.cos(third) * weights[None, :]).T
        sine = (np.sin(third) * weights[None, :]).T
        real_row = np.concatenate([cosine, sine], axis=1)
        imag_row = np.concatenate([-sine, cosine], axis=1)
        analysis = np.zeros((2 * ROWS, 2 * NZ))
        analysis[:KZ] = real_row
        analysis[ROWS : ROWS + KZ] = imag_row
        synthesis = np.zeros((2, 15 * ROWS, 2 * NZ))
        synthesis[0, 7 * ROWS : 7 * ROWS + KZ] = real_row
        synthesis[1, 7 * ROWS : 7 * ROWS + KZ] = imag_row
        depth[name] = (np.concatenate(halves(analysis), axis=0),) + halves(synthesis)
    place = first.reshape(SLAB, XP, KX)
    cosine = np.cos(place).transpose(1, 0, 2) * NORM
    sine = np.sin(place).transpose(1, 0, 2) * NORM
    rows = np.zeros((2, XP, 4, SLAB, 2, 4, KX))
    for group in range(4):
        rows[0, :, group, :, 0, group] = cosine
        rows[1, :, group, :, 0, group] = sine
        rows[0, :, group, :, 1, group] = -sine
        rows[1, :, group, :, 1, group] = cosine
    rows = rows.reshape(2 * XP * 4 * SLAB, 2 * 4 * KX)
    ty_inverse = np.concatenate([ty_inverse, np.zeros_like(ty_inverse[:, :64])], axis=1)
    flat = {}
    for name, (analysis, high, low) in depth.items():
        flat[name] = (analysis, high.reshape(-1, 2 * NZ), low.reshape(-1, 2 * NZ))
    columns = rows.T.reshape(256, 4, 256).transpose(1, 0, 2).reshape(1024, 256)
    first_part = (ty_stack, flat["plain"][0]) + halves(rows) + halves(columns) + (ty_inverse,) + flat["weighted"]
    return np.concatenate(first_part, axis=0), np.concatenate((ty_inverse,) + flat["plain"][1:], axis=0)


TY = 0
TZP = 128
XH = 192
XL = XH + 1024
IH = XL + 1024
IL = IH + 1024
TYI = IL + 1024
TZW = TYI + 128
ZWH = TZW + 64
ZWL = ZWH + 480
TABLE = ZWL + 480
LAST_TABLE = 128 + 960


def split(value):
    high = value.astype(BF16)
    low = (value - high.astype(F32)).astype(BF16)
    return high, low


def dot(left, right):
    return jnp.dot(left, right, preferred_element_type=F32)


def dot_t(left, right):
    return lax.dot_general(left, right, (((1,), (1,)), ((), ())), preferred_element_type=F32)


def cat(pieces, axis):
    return jnp.concatenate(pieces, axis=axis)


def analyse_y(pair, ty_stack, store, group):
    high, low = split(pair)
    out = dot(ty_stack[...], cat([high, low], 0))
    out = out[:64] + out[64:]
    store[pl.ds(pl.multiple_of(group * PITCH, 8), 64), :] = out[:, :NZ]
    store[pl.ds(pl.multiple_of((group + 1) * PITCH, 8), 64), :] = out[:, NZ:]


def analyse_z(store, tz_stack, sbuf, first_group, send):
    lanes = lax.broadcasted_iota(jnp.int32, (ROWS, 128), 1) < 64

    def step(turn, carry):
        group = lax.rem(first_group + turn, KY // 4)
        pieces = []
        for each in range(4):
            j = group * 4 + each
            pieces.append(cat([store[pl.ds(j, 64, stride=PITCH), :], store[pl.ds(KY + j, 64, stride=PITCH), :]], 1))
        high, low = split(cat(pieces, 0))
        out = dot_t(tz_stack[...], high)
        out = out[:32] + out[32:] + dot_t(tz_stack[:32, :], low)
        for each in range(2):
            tile = out[:, 128 * each : 128 * each + 128]
            real, imag = tile[:ROWS], tile[ROWS:]
            first = jnp.where(lanes, real, pltpu.roll(imag, 64, axis=1))
            second = jnp.where(lanes, pltpu.roll(real, 64, axis=1), imag)
            base = pl.multiple_of((group * 4 + 2 * each) * ROWS, ROWS)
            sbuf[pl.ds(base, ROWS), :] = first
            sbuf[pl.ds(base + ROWS, ROWS), :] = second
        for each in range(4):
            send(group * 4 + each)
        return carry

    lax.fori_loop(0, KY // 4, step, 0)


def analyse_x(rbuf, rows_high, rows_low):
    parts = []
    for t in range(3):
        block = cat([rbuf[pl.ds(4 * t + k, SLAB, stride=ROWS), :] for k in range(4)], 0).T
        parts.append(cat([block[16 * q : 16 * q + 16] for q in range(8)], 1))
    high, low = split(cat(parts, 0))
    out = dot(cat([high, low], 0), rows_high[...])
    return out[:48] + out[48:] + dot(high, rows_low[...])


def synthesise_x(modes, columns_high, columns_low, sbuf):
    high, low = split(modes)
    both = cat([high, low], 0)
    tiles = []
    for n in range(4):
        out = dot(both, columns_high[pl.ds(256 * n, 256), :])
        tiles.append(out[:48] + out[48:] + dot(high, columns_low[pl.ds(256 * n, 256), :]))
    out = cat(tiles, 1)
    for t in range(3):
        part = out[16 * t : 16 * t + 16]
        block = cat([part[:, 128 * q : 128 * q + 128] for q in range(8)], 0).T
        for k in range(4):
            sbuf[pl.ds(4 * t + k, SLAB, stride=ROWS), :] = block[SLAB * k : SLAB * k + SLAB]


def synthesise_z(rbuf, zi_high, zi_low, held, store):
    for g in range(4):
        block = rbuf[pl.ds(128 * g, 128), :].T
        high, low = split(cat([block[:64], block[64:]], 1))
        held[pl.ds(64 * g, 64), :] = high
        held[pl.ds(256 + 64 * g, 64), :] = low

    def step(jj, carry):
        at = pl.multiple_of(7 * ROWS - ROWS * jj, ROWS)
        table_high = cat([zi_high[pl.ds(at, 128), :], zi_high[pl.ds(at + 240, 128), :]], 0)
        table_low = cat([zi_low[pl.ds(at, 128), :], zi_low[pl.ds(at + 240, 128), :]], 0)
        out = dot(held[...], table_high)
        out = out[:256] + out[256:] + dot(held[:256, :], table_low)
        for g in range(4):
            store[pl.ds(8 * g + jj, 64, stride=PITCH), :] = out[64 * g : 64 * g + 64, :NZ]
            store[pl.ds(KY + 8 * g + jj, 64, stride=PITCH), :] = out[64 * g : 64 * g + 64, NZ:]
        return carry

    lax.fori_loop(0, 8, step, 0)


def synthesise_y(store, ty_inverse, group):
    pair = cat(
        [
            store[pl.ds(pl.multiple_of(group * PITCH, 8), 64), :],
            store[pl.ds(pl.multiple_of((group + 1) * PITCH, 8), 64), :],
        ],
        1,
    )
    high, low = split(pair)
    return dot(ty_inverse[:, :192], cat([high, low, high], 0))


def rows_of(source, x, y0):
    left = cat([source[c, x, pl.ds(y0, 8), :] for c in range(CH)], 0)
    right = cat([source[c, x, pl.ds(y0 + 8, 8), :] for c in range(CH)], 0)
    return cat([left, right], 1)


def mix_channels(kron, halves_stack, target, x, y0):
    out = dot(kron[...], halves_stack)
    out = out[:128] + out[128:]
    for c in range(CH):
        target[c, x, pl.ds(y0, 8), :] = out[8 * c : 8 * c + 8, :NZ]
        target[c, x, pl.ds(y0 + 8, 8), :] = out[8 * c : 8 * c + 8, NZ:]


def kernel(
    x_hbm, cot_hbm, w_hbm, pw_hbm, table_hbm,
    last_ref, mixed_hbm, gs_ref,
    xv, cv, bv, wv, pw, table, store, store2, held, sbuf, rbuf, vv, gv, kron1, kron2, pacc,
    vsend, vrecv, gsend, grecv, psend, precv,
    xsem, csem, wsem, pwsem, tsem, osem, ssem, rsem, vssem, vrsem, gssem, grsem, pssem, prsem,
):
    me = lax.axis_index("slab")
    mine = lax.axis_index("dp")

    def x_copy(c):
        return pltpu.make_async_copy(x_hbm.at[pl.ds(2 * c, 2)], xv.at[pl.ds(2 * c, 2)], xsem.at[c])

    def table_copy(index, start, size):
        return pltpu.make_async_copy(
            table_hbm.at[pl.ds(start, size)], table.at[pl.ds(start, size)], tsem.at[index]
        )

    first_table = table_copy(0, 0, XH)
    first_table.start()
    for c in range(CH // 2):
        x_copy(c).start()
    pw_copy = pltpu.make_async_copy(pw_hbm, pw, pwsem)
    pw_copy.start()
    second_table = table_copy(1, XH, TABLE - XH)
    second_table.start()
    w_copy = pltpu.make_async_copy(w_hbm, wv, wsem)
    w_copy.start()
    c_copy = pltpu.make_async_copy(cot_hbm, cv, csem)
    c_copy.start()

    barrier = pltpu.get_barrier_semaphore()

    def greet_slab(d, carry):
        pl.semaphore_signal(barrier, inc=1, device_id={"slab": lax.rem(me + d, SLAB)}, device_id_type=MESH)
        return carry

    def greet_dp(d, carry):
        pl.semaphore_signal(barrier, inc=1, device_id={"dp": lax.rem(mine + d, DP)}, device_id_type=MESH)
        return carry

    lax.fori_loop(1, SLAB, greet_slab, 0)
    lax.fori_loop(1, DP, greet_dp, 0)

    ty_stack = table.at[pl.ds(TY, 128)]
    tz_plain = table.at[pl.ds(TZP, 64)]
    rows_high = table.at[pl.ds(XH, 1024)]
    rows_low = table.at[pl.ds(XL, 1024)]
    columns_high = table.at[pl.ds(IH, 1024)]
    columns_low = table.at[pl.ds(IL, 1024)]
    ty_inverse = table.at[pl.ds(TYI, 128)]
    tz_weighted = table.at[pl.ds(TZW, 64)]
    zw_high = table.at[pl.ds(ZWH, 480)]
    zw_low = table.at[pl.ds(ZWL, 480)]

    def slab_copy(phase, p):
        return pltpu.make_async_remote_copy(
            src_ref=sbuf.at[phase, pl.ds(pl.multiple_of(ROWS * p, ROWS), ROWS)],
            dst_ref=rbuf.at[phase, pl.ds(pl.multiple_of(ROWS * me, ROWS), ROWS)],
            send_sem=ssem.at[phase],
            recv_sem=rsem.at[phase],
            device_id={"slab": p},
            device_id_type=MESH,
        )

    def slab_all(phase):
        every = pl.ds(0, ROWS * (SLAB - 1))
        return pltpu.make_async_remote_copy(
            src_ref=sbuf.at[phase, every],
            dst_ref=rbuf.at[phase, every],
            send_sem=ssem.at[phase],
            recv_sem=rsem.at[phase],
            device_id={"slab": lax.rem(me + 1, SLAB)},
            device_id_type=MESH,
        )

    def keep_own(phase):
        own = pl.ds(pl.multiple_of(ROWS * me, ROWS), ROWS)
        rbuf[phase, own, :] = sbuf[phase, own, :]

    def send_one(phase):
        def send(p):
            @pl.when(p != me)
            def _():
                slab_copy(phase, p).start()

            @pl.when(p == me)
            def _():
                keep_own(phase)

        return send

    def send_all(phase):
        def step(turn, carry):
            for each in range(4):
                slab_copy(phase, lax.rem(me + 16 + 4 * turn + each, SLAB)).start()
            return carry

        lax.fori_loop(0, 4, step, 0)

        def near_step(turn, carry):
            for each in range(3):
                slab_copy(phase, lax.rem(me + 1 + 3 * turn + each, SLAB)).start()
            return carry

        lax.fori_loop(0, 5, near_step, 0)
        keep_own(phase)

    first_group = me // 4 + 4

    spread = (
        lax.broadcasted_iota(jnp.int32, (128, CH), 0) // 8 == lax.broadcasted_iota(jnp.int32, (128, CH), 1)
    ).astype(F32)
    same_row = (
        lax.broadcasted_iota(jnp.int32, (128, 128), 0) % 8 == lax.broadcasted_iota(jnp.int32, (128, 128), 1) % 8
    )

    first_table.wait()

    def forward_step(c, carry):
        x_copy(c).wait()
        for x in range(XP):
            analyse_y(cat([xv[2 * c, x], xv[2 * c + 1, x]], 1), ty_stack, store, x * CH + 2 * c)
        return carry

    lax.fori_loop(0, CH // 2, forward_step, 0)
    pl.semaphore_wait(barrier, SLAB - 1 + DP - 1)
    analyse_z(store, tz_plain, sbuf.at[0], first_group, send_one(0))

    pw_copy.wait()
    wide = jnp.dot(spread, pw[...], precision=lax.Precision.HIGHEST, preferred_element_type=F32)
    wide = lax.dot_general(
        wide, spread, (((1,), (1,)), ((), ())), precision=lax.Precision.HIGHEST, preferred_element_type=F32
    )
    wide = jnp.where(same_row, wide, 0.0)
    for kron, value in ((kron1, wide.T), (kron2, wide)):
        high, low = split(value)
        kron[...] = cat([cat([high, high], 1), cat([low, jnp.zeros_like(low)], 1)], 0)
    for phase in (1, 3):
        for k in range(KZ, ROWS):
            sbuf[phase, pl.ds(k, SLAB, stride=ROWS), :] = jnp.zeros((SLAB, 128), F32)

    def mix_step(yg, carry):
        y0 = pl.multiple_of(yg * 16, 16)
        for x in range(XP):
            high, low = split(rows_of(xv, x, y0))
            mix_channels(kron1, cat([high, low], 0), bv, x, y0)
        return carry

    lax.fori_loop(0, NY // 16, mix_step, 0)
    w_copy.wait()
    second_table.wait()
    slab_all(0).wait_recv()
    modes = analyse_x(rbuf.at[0], rows_high, rows_low)
    vv[:48, :] = modes[:, :128]
    vv[48:, :] = modes[:, 128:]

    def mode_step(c, carry):
        out = []
        for t in range(3):
            wr = wv[c, :, 0, 128 * t : 128 * t + 128]
            wi = wv[c, :, 1, 128 * t : 128 * t + 128]
            vr = vv[pl.ds(16 * t + c, 1), :]
            vi = vv[pl.ds(48 + 16 * t + c, 1), :]
            out.append(carry[2 * t] + (wr * vr - wi * vi))
            out.append(carry[2 * t + 1] + (wr * vi + wi * vr))
        return tuple(out)

    mixed = lax.fori_loop(0, CH, mode_step, tuple(jnp.zeros((CH, 128), F32) for _ in range(6)))
    mixed = cat([cat([mixed[2 * t], mixed[2 * t + 1]], 1) for t in range(3)], 0)
    synthesise_x(mixed, columns_high, columns_low, sbuf.at[1])
    send_all(1)

    def v_copy(d):
        return pltpu.make_async_remote_copy(
            src_ref=vsend.at[pl.ds(pl.multiple_of(16 * d, 16), 16)],
            dst_ref=vrecv.at[pl.ds(pl.multiple_of(16 * mine, 16), 16)],
            send_sem=vssem,
            recv_sem=vrsem,
            device_id={"dp": d},
            device_id_type=MESH,
        )

    vsend[...] = jnp.zeros_like(vsend)
    for d in range(DP):
        for c in range(2):
            for t in range(3):
                row = 16 * t + 2 * d + c
                at = 16 * d + 6 * c + t
                vsend[at : at + 1, :] = vv[row : row + 1, :]
                vsend[at + 3 : at + 4, :] = vv[row + 48 : row + 49, :]

    def v_send(d, carry):
        v_copy(lax.rem(mine + d, DP)).start()
        return carry

    lax.fori_loop(1, DP, v_send, 0)
    own_v = pl.ds(pl.multiple_of(16 * mine, 16), 16)
    vrecv[own_v, :] = vsend[own_v, :]

    c_copy.wait()
    slab_all(1).wait_recv()

    synthesise_z(rbuf.at[1], zw_high, zw_low, held, store)

    def middle_step(o, carry):
        for x in range(XP):
            carried = synthesise_y(store, ty_inverse, x * CH + 2 * o)
            grads = []
            for each in range(2):
                before = carried[:, NZ * each : NZ * each + NZ] + bv[2 * o + each, x]
                slope = 0.5 * (1.0 + lax.erf(before * (1.0 / math.sqrt(2.0)))) + before * jnp.exp(
                    -0.5 * before * before
                ) * (1.0 / math.sqrt(2.0 * math.pi))
                grad = cv[2 * o + each, x] * slope
                cv[2 * o + each, x] = grad
                grads.append(grad)
            analyse_y(cat(grads, 1), ty_stack, store2, x * CH + 2 * o)
        return carry

    lax.fori_loop(0, CH // 2, middle_step, 0)
    analyse_z(store2, tz_weighted, sbuf.at[2], first_group, send_one(2))

    pacc[...] = jnp.zeros_like(pacc)

    def back_step(yg, carry):
        y0 = pl.multiple_of(yg * 16, 16)
        for x in range(XP):
            high, low = split(rows_of(cv, x, y0))
            stack = cat([high, low], 0)
            mix_channels(kron2, stack, bv, x, y0)
            xhigh, xlow = split(rows_of(xv, x, y0))
            pacc[...] += dot_t(cat([xhigh, xlow], 0), stack)
        return carry

    lax.fori_loop(0, NY // 16, back_step, 0)
    o_copy = pltpu.make_async_copy(bv, mixed_hbm, osem)
    o_copy.start()
    part = pacc[:128, :128] + pacc[:128, 128:] + pacc[128:, :128] + pacc[128:, 128:]
    part = jnp.where(same_row, part, 0.0)
    part = jnp.dot(part, spread, precision=lax.Precision.HIGHEST, preferred_element_type=F32)
    part = lax.dot_general(
        spread, part, (((0,), (0,)), ((), ())), precision=lax.Precision.HIGHEST, preferred_element_type=F32
    )
    part = cat([part, jnp.zeros((CH, 128 - CH), F32)], 1)

    def p_copy(d):
        return pltpu.make_async_remote_copy(
            src_ref=psend,
            dst_ref=precv.at[pl.ds(pl.multiple_of(16 * mine, 16), 16)],
            send_sem=pssem,
            recv_sem=prsem,
            device_id={"dp": d},
            device_id_type=MESH,
        )

    psend[...] = part

    def p_send(d, carry):
        p_copy(lax.rem(mine + d, DP)).start()
        return carry

    lax.fori_loop(1, DP, p_send, 0)
    precv[pl.ds(pl.multiple_of(16 * mine, 16), 16), :] = part

    slab_all(2).wait_recv()
    modes = analyse_x(rbuf.at[2], rows_high, rows_low)
    gv[:48, :] = modes[:, :128]
    gv[48:, :] = modes[:, 128:]

    def back_mode_step(c, carry):
        for t in range(3):
            wr = wv[c, :, 0, 128 * t : 128 * t + 128]
            wi = wv[c, :, 1, 128 * t : 128 * t + 128]
            gr = gv[16 * t : 16 * t + 16, :]
            gi = gv[48 + 16 * t : 64 + 16 * t, :]
            vv[pl.ds(16 * t + c, 1), :] = jnp.sum(wr * gr + wi * gi, axis=0, keepdims=True)
            vv[pl.ds(48 + 16 * t + c, 1), :] = jnp.sum(wr * gi - wi * gr, axis=0, keepdims=True)
        return carry

    lax.fori_loop(0, CH, back_mode_step, 0)

    def dp_all(source, target, size, send_sem, recv_sem):
        return pltpu.make_async_remote_copy(
            src_ref=source.at[pl.ds(0, size)],
            dst_ref=target.at[pl.ds(0, size)],
            send_sem=send_sem,
            recv_sem=recv_sem,
            device_id={"dp": lax.rem(mine + 1, DP)},
            device_id_type=MESH,
        )

    p_all = dp_all(precv, precv, 16 * (DP - 1), pssem, prsem)
    v_all = dp_all(vrecv, vrecv, 16 * (DP - 1), vssem, vrsem)
    g_all = dp_all(grecv, grecv, 96 * (DP - 1), gssem, grsem)
    p_all.wait_recv()
    total = precv[0:16, :]
    for d in range(1, DP):
        total = total + precv[16 * d : 16 * d + 16, :]
    for r in range(2):
        flat = cat([total[8 * r + i : 8 * r + i + 1, :CH] for i in range(8)], 1)
        sbuf[3, pl.ds(KZ + r, SLAB, stride=ROWS), :] = jnp.broadcast_to(flat, (SLAB, 128))
    synthesise_x(cat([vv[:48, :], vv[48:, :]], 1), columns_high, columns_low, sbuf.at[3])
    send_all(3)

    def g_copy(d):
        return pltpu.make_async_remote_copy(
            src_ref=gsend,
            dst_ref=grecv.at[pl.ds(pl.multiple_of(96 * mine, 16), 96)],
            send_sem=gssem,
            recv_sem=grsem,
            device_id={"dp": d},
            device_id_type=MESH,
        )

    gsend[...] = gv[...]

    def g_send(d, carry):
        g_copy(lax.rem(mine + d, DP)).start()
        return carry

    lax.fori_loop(1, DP, g_send, 0)
    grecv[pl.ds(pl.multiple_of(96 * mine, 16), 96), :] = gv[...]
    v_all.wait_recv()
    g_all.wait_recv()

    for c in range(2):
        def sample_step(d, carry):
            out = []
            base = pl.multiple_of(96 * d, 16)
            for t in range(3):
                vr = vrecv[pl.ds(16 * d + 6 * c + t, 1), :]
                vi = vrecv[pl.ds(16 * d + 6 * c + 3 + t, 1), :]
                gr = grecv[pl.ds(base + 16 * t, 16), :]
                gi = grecv[pl.ds(base + 48 + 16 * t, 16), :]
                out.append(carry[2 * t] + (gr * vr + gi * vi))
                out.append(carry[2 * t + 1] + (gi * vr - gr * vi))
            return tuple(out)

        total = lax.fori_loop(0, DP, sample_step, tuple(jnp.zeros((CH, 128), F32) for _ in range(6)))
        for t in range(3):
            gs_ref[c, :, 0, 128 * t : 128 * t + 128] = total[2 * t]
            gs_ref[c, :, 1, 128 * t : 128 * t + 128] = total[2 * t + 1]

    slab_all(3).wait_recv()
    last_ref[...] = rbuf[3]

    for phase in range(4):
        slab_all(phase).wait_send()
    p_out = pltpu.make_async_remote_copy(
        src_ref=precv.at[pl.ds(0, 16 * (DP - 1))],
        dst_ref=precv.at[pl.ds(0, 16 * (DP - 1))],
        send_sem=pssem,
        recv_sem=prsem,
        device_id={"dp": lax.rem(mine + 1, DP)},
        device_id_type=MESH,
    )
    p_out.wait_send()
    v_all.wait_send()
    g_all.wait_send()
    o_copy.wait()


def last_kernel(
    rows_hbm, mixed_hbm, gs_in, table_hbm, gi_hbm, gs_hbm, gp_hbm,
    rows_ref, gs_ref, bv, table, held, store, gp, insem, tsem, osem, gssem, gpsem, rsem,
):
    rows_copy = pltpu.make_async_copy(rows_hbm, rows_ref, rsem)
    rows_copy.start()
    table_copy = pltpu.make_async_copy(table_hbm, table, tsem)
    table_copy.start()

    def in_copy(c):
        return pltpu.make_async_copy(mixed_hbm.at[pl.ds(2 * c, 2)], bv.at[pl.ds(2 * c, 2)], insem.at[c])

    def out_copy(c):
        return pltpu.make_async_copy(bv.at[pl.ds(2 * c, 2)], gi_hbm.at[pl.ds(2 * c, 2)], osem.at[c])

    for c in range(CH // 2):
        in_copy(c).start()
    gs_load = pltpu.make_async_copy(gs_in, gs_ref, gssem)
    gs_load.start()
    rows_copy.wait()
    for r in range(2):
        flat = jnp.sum(rows_ref[pl.ds(KZ + r, SLAB, stride=ROWS), :], axis=0, keepdims=True)
        for i in range(8):
            gp[8 * r + i : 8 * r + i + 1, :] = flat[:, CH * i : CH * i + CH] * (1.0 / math.sqrt(DP * NX * NY * NZ))
    gp_copy = pltpu.make_async_copy(gp, gp_hbm, gpsem)
    gp_copy.start()
    table_copy.wait()
    ty_inverse = table.at[pl.ds(0, 128)]
    synthesise_z(rows_ref, table.at[pl.ds(128, 480)], table.at[pl.ds(608, 480)], held, store)

    def last_step(c, carry):
        in_copy(c).wait()
        for x in range(XP):
            out = synthesise_y(store, ty_inverse, x * CH + 2 * c)
            bv[2 * c, x] = bv[2 * c, x] + out[:, :NZ]
            bv[2 * c + 1, x] = bv[2 * c + 1, x] + out[:, NZ:]
        out_copy(c).start()
        return carry

    gs_load.wait()
    gs_copy = pltpu.make_async_copy(gs_ref, gs_hbm, gssem)
    gs_copy.start()
    lax.fori_loop(0, CH // 2, last_step, 0)
    gs_copy.wait()
    gp_copy.wait()
    for c in range(CH // 2):
        out_copy(c).wait()


def body(inputs, cotangent, spectral_weights, pointwise_weights):
    main_table, last_table = (jnp.asarray(table) for table in tables())
    hbm = pl.BlockSpec(memory_space=pltpu.HBM)
    vmem = pl.BlockSpec(memory_space=pltpu.VMEM)
    block = (CH, XP, NY, NZ)
    dma = pltpu.SemaphoreType.DMA
    block_shape = jax.ShapeDtypeStruct(block, F32)
    weight_shape = jax.ShapeDtypeStruct((2, CH, 2, KX * KZ), F32)
    store_shape = pltpu.VMEM((CH * XP * PITCH, NZ), F32)
    rows, mixed, weight_part = pl.pallas_call(
        kernel,
        out_shape=[jax.ShapeDtypeStruct((SLAB * ROWS, 128), F32), block_shape, weight_shape],
        in_specs=[hbm] * 5,
        out_specs=[vmem, hbm, vmem],
        scratch_shapes=[
            pltpu.VMEM(block, F32),
            pltpu.VMEM(block, F32),
            pltpu.VMEM(block, F32),
            pltpu.VMEM((CH, CH, 2, KX * KZ), F32),
            pltpu.VMEM((CH, CH), F32),
            pltpu.VMEM((TABLE, 256), BF16),
            store_shape,
            store_shape,
            pltpu.VMEM((512, 256), BF16),
            pltpu.VMEM((4, SLAB * ROWS, 128), F32),
            pltpu.VMEM((4, SLAB * ROWS, 128), F32),
            pltpu.VMEM((96, 128), F32),
            pltpu.VMEM((96, 128), F32),
            pltpu.VMEM((256, 256), BF16),
            pltpu.VMEM((256, 256), BF16),
            pltpu.VMEM((256, 256), F32),
            pltpu.VMEM((16 * DP, 128), F32),
            pltpu.VMEM((16 * DP, 128), F32),
            pltpu.VMEM((96, 128), F32),
            pltpu.VMEM((96 * DP, 128), F32),
            pltpu.VMEM((16, 128), F32),
            pltpu.VMEM((16 * DP, 128), F32),
            dma((CH // 2,)),
            dma,
            dma,
            dma,
            dma((2,)),
            dma,
            dma((4,)),
            dma((4,)),
            dma,
            dma,
            dma,
            dma,
            dma,
            dma,
        ],
        compiler_params=pltpu.CompilerParams(
            collective_id=0, has_side_effects=True, vmem_limit_bytes=60 * 1024 * 1024
        ),
        name="layer_backward",
    )(inputs.reshape(block), cotangent.reshape(block), spectral_weights, pointwise_weights, main_table)
    grad_inputs, grad_spectral, grad_pointwise = pl.pallas_call(
        last_kernel,
        out_shape=[block_shape, weight_shape, jax.ShapeDtypeStruct((CH, CH), F32)],
        in_specs=[hbm] * 4,
        out_specs=[hbm, hbm, hbm],
        scratch_shapes=[
            pltpu.VMEM((SLAB * ROWS, 128), F32),
            pltpu.VMEM((2, CH, 2, KX * KZ), F32),
            pltpu.VMEM(block, F32),
            pltpu.VMEM((LAST_TABLE, 256), BF16),
            pltpu.VMEM((512, 256), BF16),
            store_shape,
            pltpu.VMEM((CH, CH), F32),
            dma((CH // 2,)),
            dma,
            dma((CH // 2,)),
            dma,
            dma,
            dma,
        ],
        compiler_params=pltpu.CompilerParams(vmem_limit_bytes=60 * 1024 * 1024),
        name="input_gradient",
    )(rows, mixed, weight_part, last_table)
    return (grad_inputs[None], grad_spectral, grad_pointwise)


def solution(mesh):
    placed = (
        P("dp", None, "slab", None, None),
        P("dp", None, "slab", None, None),
        P(None, None, None, "slab"),
        P(),
    )
    return jax.shard_map(
        body,
        mesh=mesh,
        in_specs=placed,
        out_specs=(P("dp", None, "slab", None, None), P("dp", None, None, "slab"), P()),
        check_vma=False,
    )
```

time: 104 us -> 78.4 us (0.75)
  the two profiles are of different devices: /device:TPU:99 before, /device:TPU:1 now
where the time goes in v2:
time: 78.4 us
  Pallas kernels  77.7 us (99%)
    pallas_call x1, Pallas kernels, body(): pl.pallas_call(kernel, out_shape=[jax.ShapeDtypeStruct((SLAB * ROWS, 128)...  70.2 us
    pallas_call x1, Pallas kernels, body(): pl.pallas_call(last_kernel, out_shape=[block_shape, weight_shape, jax.Sha...  7.47 us

profile of v2, /device:TPU:1, one launch (start us, length us, event | category | flops | bytes accessed | tf_op | source)
XLA Modules:
  0.0 78.4 jit_solution(16500131247618002065)
XLA Ops:
  0.6 70.2 %layer_backward.1 = (f32[512,128]{1,0:T(8,128)}, f32[16,4,128,128]{3,2,1,0:T(8,128)}, f32[2,16,2,384]{3,2,1,0:T(2,128)}) custom-call(f32[16,4,128,128]{3,2,1,0:T(8,128)} %bitcast.3, f32[16,4,128,128]{3,2,1,0:T(8,128)} %bitcast.4, f32[16,16,2,384]{3,2,1,0:T(2,128)} %w_hbm.1, f32[16,16]{1,0:T(8,128)} %pw_hbm.1, bf16[5440,256]{1,0:T(8,128)(2,1)} %constant.4.clone.table_hbm), custom_call_target="tpu_custom_call" | custom-call | tf_op jit(solution)/shard_map/layer_backward/pallas_call | solution.py:648
  70.9 7.5 %input_gradient.1 = (f32[16,4,128,128]{3,2,1,0:T(8,128)}, f32[2,16,2,384]{3,2,1,0:T(2,128)}, f32[16,16]{1,0:T(8,128)}) custom-call(f32[512,128]{1,0:T(8,128)} %get-tuple-element.9.rows_hbm, f32[16,4,128,128]{3,2,1,0:T(8,128)} %get-tuple-element.10.mixed_hbm, f32[2,16,2,384]{3,2,1,0:T(2,128)} %get-tuple-element.11.gs_in, ...), custom_call_target="tpu_custom_call" | custom-call | tf_op jit(solution)/shard_map/input_gradient/pallas_call | solution.py:696

commit v3 on v2

--- a/solution.py
+++ b/solution.py
@@ -125,7 +125,7 @@
     store[pl.ds(pl.multiple_of((group + 1) * PITCH, 8), 64), :] = out[:, NZ:]
 
 
-def analyse_z(store, tz_stack, sbuf, first_group, send):
+def analyse_z(store, tz_stack, sbuf, phase, first_group, send):
     lanes = lax.broadcasted_iota(jnp.int32, (ROWS, 128), 1) < 64
 
     def step(turn, carry):
@@ -142,9 +142,8 @@
             real, imag = tile[:ROWS], tile[ROWS:]
             first = jnp.where(lanes, real, pltpu.roll(imag, 64, axis=1))
             second = jnp.where(lanes, pltpu.roll(real, 64, axis=1), imag)
-            base = pl.multiple_of((group * 4 + 2 * each) * ROWS, ROWS)
-            sbuf[pl.ds(base, ROWS), :] = first
-            sbuf[pl.ds(base + ROWS, ROWS), :] = second
+            sbuf[phase, group * 4 + 2 * each] = first[:KZ]
+            sbuf[phase, group * 4 + 2 * each + 1] = second[:KZ]
         for each in range(4):
             send(group * 4 + each)
         return carry
@@ -152,17 +151,17 @@
     lax.fori_loop(0, KY // 4, step, 0)
 
 
-def analyse_x(rbuf, rows_high, rows_low):
+def analyse_x(rbuf, phase, rows_high, rows_low):
     parts = []
     for t in range(3):
-        block = cat([rbuf[pl.ds(4 * t + k, SLAB, stride=ROWS), :] for k in range(4)], 0).T
+        block = cat([rbuf[phase, :, 4 * t + k, :] for k in range(4)], 0).T
         parts.append(cat([block[16 * q : 16 * q + 16] for q in range(8)], 1))
     high, low = split(cat(parts, 0))
     out = dot(cat([high, low], 0), rows_high[...])
     return out[:48] + out[48:] + dot(high, rows_low[...])
 
 
-def synthesise_x(modes, columns_high, columns_low, sbuf):
+def synthesise_x(modes, columns_high, columns_low, put):
     high, low = split(modes)
     both = cat([high, low], 0)
     tiles = []
@@ -174,12 +173,12 @@
         part = out[16 * t : 16 * t + 16]
         block = cat([part[:, 128 * q : 128 * q + 128] for q in range(8)], 0).T
         for k in range(4):
-            sbuf[pl.ds(4 * t + k, SLAB, stride=ROWS), :] = block[SLAB * k : SLAB * k + SLAB]
-
-
-def synthesise_z(rbuf, zi_high, zi_low, held, store):
+            put(4 * t + k, block[SLAB * k : SLAB * k + SLAB])
+
+
+def synthesise_z(block_of, zi_high, zi_low, held, store):
     for g in range(4):
-        block = rbuf[pl.ds(128 * g, 128), :].T
+        block = block_of(g).T
         high, low = split(cat([block[:64], block[64:]], 1))
         held[pl.ds(64 * g, 64), :] = high
         held[pl.ds(256 + 64 * g, 64), :] = low
@@ -227,9 +226,9 @@
 def kernel(
     x_hbm, cot_hbm, w_hbm, pw_hbm, table_hbm,
     last_ref, mixed_hbm, gs_ref,
-    xv, cv, bv, wv, pw, table, store, store2, held, sbuf, rbuf, vv, gv, kron1, kron2, pacc,
-    vsend, vrecv, gsend, grecv, psend, precv,
-    xsem, csem, wsem, pwsem, tsem, osem, ssem, rsem, vssem, vrsem, gssem, grsem, pssem, prsem,
+    xv, cv, bv, wv, wco, woc, pw, table, store, store2, held, sbuf, rbuf, sbuf3, rbuf3, vv, gv, kron1, kron2, pacc,
+    vsend, vrecv, grecv, psend, precv,
+    xsem, csem, wsem, pwsem, tsem, osem, ssem, rsem, vssem, vrsem, gssem, grsem, hssem, hrsem, pssem, prsem,
 ):
     me = lax.axis_index("slab")
     mine = lax.axis_index("dp")
@@ -279,10 +278,20 @@
     zw_high = table.at[pl.ds(ZWH, 480)]
     zw_low = table.at[pl.ds(ZWL, 480)]
 
+    def source(phase, p):
+        if phase == 3:
+            return sbuf3.at[pl.ds(pl.multiple_of(ROWS * p, ROWS), ROWS)]
+        return sbuf.at[phase, p]
+
+    def target(phase, p):
+        if phase == 3:
+            return rbuf3.at[pl.ds(pl.multiple_of(ROWS * p, ROWS), ROWS)]
+        return rbuf.at[phase, p]
+
     def slab_copy(phase, p):
         return pltpu.make_async_remote_copy(
-            src_ref=sbuf.at[phase, pl.ds(pl.multiple_of(ROWS * p, ROWS), ROWS)],
-            dst_ref=rbuf.at[phase, pl.ds(pl.multiple_of(ROWS * me, ROWS), ROWS)],
+            src_ref=source(phase, p),
+            dst_ref=target(phase, me),
             send_sem=ssem.at[phase],
             recv_sem=rsem.at[phase],
             device_id={"slab": p},
@@ -290,10 +299,15 @@
         )
 
     def slab_all(phase):
-        every = pl.ds(0, ROWS * (SLAB - 1))
+        if phase == 3:
+            every = pl.ds(0, ROWS * (SLAB - 1))
+            src, dst = sbuf3.at[every], rbuf3.at[every]
+        else:
+            every = pl.ds(0, SLAB - 1)
+            src, dst = sbuf.at[phase, every], rbuf.at[phase, every]
         return pltpu.make_async_remote_copy(
-            src_ref=sbuf.at[phase, every],
-            dst_ref=rbuf.at[phase, every],
+            src_ref=src,
+            dst_ref=dst,
             send_sem=ssem.at[phase],
             recv_sem=rsem.at[phase],
             device_id={"slab": lax.rem(me + 1, SLAB)},
@@ -301,8 +315,11 @@
         )
 
     def keep_own(phase):
-        own = pl.ds(pl.multiple_of(ROWS * me, ROWS), ROWS)
-        rbuf[phase, own, :] = sbuf[phase, own, :]
+        if phase == 3:
+            own = pl.ds(pl.multiple_of(ROWS * me, ROWS), ROWS)
+            rbuf3[own, :] = sbuf3[own, :]
+        else:
+            rbuf[phase, me] = sbuf[phase, me]
 
     def send_one(phase):
         def send(p):
@@ -333,6 +350,8 @@
         keep_own(phase)
 
     first_group = me // 4 + 4
+    core = lax.rem(mine, 2)
+    place = core * 4 + mine // 2
 
     spread = (
         lax.broadcasted_iota(jnp.int32, (128, CH), 0) // 8 == lax.broadcasted_iota(jnp.int32, (128, CH), 1)
@@ -351,7 +370,7 @@
 
     lax.fori_loop(0, CH // 2, forward_step, 0)
     pl.semaphore_wait(barrier, SLAB - 1 + DP - 1)
-    analyse_z(store, tz_plain, sbuf.at[0], first_group, send_one(0))
+    analyse_z(store, tz_plain, sbuf, 0, first_group, send_one(0))
 
     pw_copy.wait()
     wide = jnp.dot(spread, pw[...], precision=lax.Precision.HIGHEST, preferred_element_type=F32)
@@ -362,9 +381,8 @@
     for kron, value in ((kron1, wide.T), (kron2, wide)):
         high, low = split(value)
         kron[...] = cat([cat([high, high], 1), cat([low, jnp.zeros_like(low)], 1)], 0)
-    for phase in (1, 3):
-        for k in range(KZ, ROWS):
-            sbuf[phase, pl.ds(k, SLAB, stride=ROWS), :] = jnp.zeros((SLAB, 128), F32)
+    for k in range(KZ + 2, ROWS):
+        sbuf3[pl.ds(k, SLAB, stride=ROWS), :] = jnp.zeros((SLAB, 128), F32)
 
     def mix_step(yg, carry):
         y0 = pl.multiple_of(yg * 16, 16)
@@ -375,32 +393,45 @@
 
     lax.fori_loop(0, NY // 16, mix_step, 0)
     w_copy.wait()
+
+    def regroup_step(c, carry):
+        base = pl.multiple_of(c * 96, 16)
+        for ri in range(2):
+            for t in range(3):
+                wco[pl.ds(base + 48 * ri + 16 * t, 16), :] = wv[c, :, ri, 128 * t : 128 * t + 128]
+        return carry
+
+    lax.fori_loop(0, CH, regroup_step, 0)
     second_table.wait()
     slab_all(0).wait_recv()
-    modes = analyse_x(rbuf.at[0], rows_high, rows_low)
+    modes = analyse_x(rbuf, 0, rows_high, rows_low)
     vv[:48, :] = modes[:, :128]
     vv[48:, :] = modes[:, 128:]
 
+    def spread_row(modes, c):
+        return cat([jnp.broadcast_to(modes[pl.ds(16 * t + c, 1), :], (16, 128)) for t in range(3)], 0), cat(
+            [jnp.broadcast_to(modes[pl.ds(48 + 16 * t + c, 1), :], (16, 128)) for t in range(3)], 0
+        )
+
     def mode_step(c, carry):
-        out = []
-        for t in range(3):
-            wr = wv[c, :, 0, 128 * t : 128 * t + 128]
-            wi = wv[c, :, 1, 128 * t : 128 * t + 128]
-            vr = vv[pl.ds(16 * t + c, 1), :]
-            vi = vv[pl.ds(48 + 16 * t + c, 1), :]
-            out.append(carry[2 * t] + (wr * vr - wi * vi))
-            out.append(carry[2 * t + 1] + (wr * vi + wi * vr))
-        return tuple(out)
-
-    mixed = lax.fori_loop(0, CH, mode_step, tuple(jnp.zeros((CH, 128), F32) for _ in range(6)))
-    mixed = cat([cat([mixed[2 * t], mixed[2 * t + 1]], 1) for t in range(3)], 0)
-    synthesise_x(mixed, columns_high, columns_low, sbuf.at[1])
+        base = pl.multiple_of(c * 96, 16)
+        wr, wi = wco[pl.ds(base, 48), :], wco[pl.ds(base + 48, 48), :]
+        vr, vi = spread_row(vv, c)
+        return carry[0] + (wr * vr - wi * vi), carry[1] + (wr * vi + wi * vr)
+
+    no_modes = (jnp.zeros((48, 128), F32), jnp.zeros((48, 128), F32))
+    mixed = cat(lax.fori_loop(0, CH, mode_step, no_modes), 1)
+
+    def put_mixed(k, value):
+        sbuf[1, :, k, :] = value
+
+    synthesise_x(mixed, columns_high, columns_low, put_mixed)
     send_all(1)
 
     def v_copy(d):
         return pltpu.make_async_remote_copy(
             src_ref=vsend.at[pl.ds(pl.multiple_of(16 * d, 16), 16)],
-            dst_ref=vrecv.at[pl.ds(pl.multiple_of(16 * mine, 16), 16)],
+            dst_ref=vrecv.at[pl.ds(pl.multiple_of(16 * place, 16), 16)],
             send_sem=vssem,
             recv_sem=vrsem,
             device_id={"dp": d},
@@ -421,13 +452,27 @@
         return carry
 
     lax.fori_loop(1, DP, v_send, 0)
-    own_v = pl.ds(pl.multiple_of(16 * mine, 16), 16)
-    vrecv[own_v, :] = vsend[own_v, :]
+    vrecv[pl.ds(pl.multiple_of(16 * place, 16), 16), :] = vsend[pl.ds(pl.multiple_of(16 * mine, 16), 16), :]
+
+    def turn_step(o, carry):
+        base = pl.multiple_of(o * 96, 16)
+        for part in range(6):
+            woc[pl.ds(base + 16 * part, 16), :] = wco[pl.ds(16 * part + o, 16, stride=96), :]
+        return carry
+
+    lax.fori_loop(0, CH, turn_step, 0)
 
     c_copy.wait()
     slab_all(1).wait_recv()
 
-    synthesise_z(rbuf.at[1], zw_high, zw_low, held, store)
+    def block_of(g):
+        spare = jnp.zeros((ROWS - KZ, 128), F32)
+        pieces = []
+        for each in range(8):
+            pieces += [rbuf[1, 8 * g + each], spare]
+        return cat(pieces, 0)
+
+    synthesise_z(block_of, zw_high, zw_low, held, store)
 
     def middle_step(o, carry):
         for x in range(XP):
@@ -445,7 +490,7 @@
         return carry
 
     lax.fori_loop(0, CH // 2, middle_step, 0)
-    analyse_z(store2, tz_weighted, sbuf.at[2], first_group, send_one(2))
+    analyse_z(store2, tz_weighted, sbuf, 2, first_group, send_one(2))
 
     pacc[...] = jnp.zeros_like(pacc)
 
@@ -468,12 +513,13 @@
     part = lax.dot_general(
         spread, part, (((0,), (0,)), ((), ())), precision=lax.Precision.HIGHEST, preferred_element_type=F32
     )
-    part = cat([part, jnp.zeros((CH, 128 - CH), F32)], 1)
+    flat = [cat([part[8 * r + i : 8 * r + i + 1, :] for i in range(8)], 1) for r in range(2)]
+    part = cat(flat + [jnp.zeros((6, 128), F32)], 0)
 
     def p_copy(d):
         return pltpu.make_async_remote_copy(
             src_ref=psend,
-            dst_ref=precv.at[pl.ds(pl.multiple_of(16 * mine, 16), 16)],
+            dst_ref=precv.at[pl.ds(pl.multiple_of(8 * mine, 8), 8)],
             send_sem=pssem,
             recv_sem=prsem,
             device_id={"dp": d},
@@ -487,24 +533,23 @@
         return carry
 
     lax.fori_loop(1, DP, p_send, 0)
-    precv[pl.ds(pl.multiple_of(16 * mine, 16), 16), :] = part
+    precv[pl.ds(pl.multiple_of(8 * mine, 8), 8), :] = part
 
     slab_all(2).wait_recv()
-    modes = analyse_x(rbuf.at[2], rows_high, rows_low)
+    modes = analyse_x(rbuf, 2, rows_high, rows_low)
     gv[:48, :] = modes[:, :128]
     gv[48:, :] = modes[:, 128:]
 
-    def back_mode_step(c, carry):
-        for t in range(3):
-            wr = wv[c, :, 0, 128 * t : 128 * t + 128]
-            wi = wv[c, :, 1, 128 * t : 128 * t + 128]
-            gr = gv[16 * t : 16 * t + 16, :]
-            gi = gv[48 + 16 * t : 64 + 16 * t, :]
-            vv[pl.ds(16 * t + c, 1), :] = jnp.sum(wr * gr + wi * gi, axis=0, keepdims=True)
-            vv[pl.ds(48 + 16 * t + c, 1), :] = jnp.sum(wr * gi - wi * gr, axis=0, keepdims=True)
-        return carry
-
-    lax.fori_loop(0, CH, back_mode_step, 0)
+    def back_mode_step(o, carry):
+        base = pl.multiple_of(o * 96, 16)
+        wr, wi = woc[pl.ds(base, 48), :], woc[pl.ds(base + 48, 48), :]
+        gr, gi = spread_row(gv, o)
+        return carry[0] + (wr * gr + wi * gi), carry[1] + (wr * gi - wi * gr)
+
+    back = cat(lax.fori_loop(0, CH, back_mode_step, no_modes), 1)
+
+    def put_back(k, value):
+        sbuf3[pl.ds(k, SLAB, stride=ROWS), :] = value
 
     def dp_all(source, target, size, send_sem, recv_sem):
         return pltpu.make_async_remote_copy(
@@ -516,39 +561,46 @@
             device_id_type=MESH,
         )
 
-    p_all = dp_all(precv, precv, 16 * (DP - 1), pssem, prsem)
+    p_all = dp_all(precv, precv, 8 * (DP - 1), pssem, prsem)
     v_all = dp_all(vrecv, vrecv, 16 * (DP - 1), vssem, vrsem)
-    g_all = dp_all(grecv, grecv, 96 * (DP - 1), gssem, grsem)
+    g_all = dp_all(grecv, grecv, 96 * 3, gssem, grsem)
     p_all.wait_recv()
-    total = precv[0:16, :]
+    total = precv[0:8, :]
     for d in range(1, DP):
-        total = total + precv[16 * d : 16 * d + 16, :]
+        total = total + precv[8 * d : 8 * d + 8, :]
     for r in range(2):
-        flat = cat([total[8 * r + i : 8 * r + i + 1, :CH] for i in range(8)], 1)
-        sbuf[3, pl.ds(KZ + r, SLAB, stride=ROWS), :] = jnp.broadcast_to(flat, (SLAB, 128))
-    synthesise_x(cat([vv[:48, :], vv[48:, :]], 1), columns_high, columns_low, sbuf.at[3])
+        sbuf3[pl.ds(KZ + r, SLAB, stride=ROWS), :] = jnp.broadcast_to(total[r : r + 1, :], (SLAB, 128))
+    synthesise_x(back, columns_high, columns_low, put_back)
     send_all(3)
 
     def g_copy(d):
         return pltpu.make_async_remote_copy(
-            src_ref=gsend,
-            dst_ref=grecv.at[pl.ds(pl.multiple_of(96 * mine, 16), 96)],
+            src_ref=gv,
+            dst_ref=grecv.at[pl.ds(pl.multiple_of(96 * place, 16), 96)],
             send_sem=gssem,
             recv_sem=grsem,
-            device_id={"dp": d},
+            device_id={"dp": lax.rem(mine + 2 * d, DP)},
             device_id_type=MESH,
         )
 
-    gsend[...] = gv[...]
-
-    def g_send(d, carry):
-        g_copy(lax.rem(mine + d, DP)).start()
-        return carry
-
-    lax.fori_loop(1, DP, g_send, 0)
-    grecv[pl.ds(pl.multiple_of(96 * mine, 16), 96), :] = gv[...]
+    for d in range(1, 4):
+        g_copy(d).start()
+    grecv[pl.ds(pl.multiple_of(96 * place, 16), 96), :] = gv[...]
     v_all.wait_recv()
     g_all.wait_recv()
+    half = pl.ds(pl.multiple_of(core * 384, 16), 384)
+    h_copy = pltpu.make_async_remote_copy(
+        src_ref=grecv.at[half],
+        dst_ref=grecv.at[half],
+        send_sem=hssem,
+        recv_sem=hrsem,
+        device_id={"dp": mine + 1 - 2 * core},
+        device_id_type=MESH,
+    )
+    h_copy.start()
+    slab_all(3).wait_recv()
+    last_ref[...] = rbuf3[...]
+    h_copy.wait()
 
     for c in range(2):
         def sample_step(d, carry):
@@ -568,20 +620,9 @@
             gs_ref[c, :, 0, 128 * t : 128 * t + 128] = total[2 * t]
             gs_ref[c, :, 1, 128 * t : 128 * t + 128] = total[2 * t + 1]
 
-    slab_all(3).wait_recv()
-    last_ref[...] = rbuf[3]
-
     for phase in range(4):
         slab_all(phase).wait_send()
-    p_out = pltpu.make_async_remote_copy(
-        src_ref=precv.at[pl.ds(0, 16 * (DP - 1))],
-        dst_ref=precv.at[pl.ds(0, 16 * (DP - 1))],
-        send_sem=pssem,
-        recv_sem=prsem,
-        device_id={"dp": lax.rem(mine + 1, DP)},
-        device_id_type=MESH,
-    )
-    p_out.wait_send()
+    p_all.wait_send()
     v_all.wait_send()
     g_all.wait_send()
     o_copy.wait()
@@ -615,7 +656,7 @@
     gp_copy.start()
     table_copy.wait()
     ty_inverse = table.at[pl.ds(0, 128)]
-    synthesise_z(rows_ref, table.at[pl.ds(128, 480)], table.at[pl.ds(608, 480)], held, store)
+    synthesise_z(lambda g: rows_ref[pl.ds(128 * g, 128), :], table.at[pl.ds(128, 480)], table.at[pl.ds(608, 480)], held, store)
 
     def last_step(c, carry):
         in_copy(c).wait()
@@ -655,13 +696,17 @@
             pltpu.VMEM(block, F32),
             pltpu.VMEM(block, F32),
             pltpu.VMEM((CH, CH, 2, KX * KZ), F32),
+            pltpu.VMEM((CH * 96, 128), F32),
+            pltpu.VMEM((CH * 96, 128), F32),
             pltpu.VMEM((CH, CH), F32),
             pltpu.VMEM((TABLE, 256), BF16),
             store_shape,
             store_shape,
             pltpu.VMEM((512, 256), BF16),
-            pltpu.VMEM((4, SLAB * ROWS, 128), F32),
-            pltpu.VMEM((4, SLAB * ROWS, 128), F32),
+            pltpu.VMEM((3, SLAB, KZ, 128), F32),
+            pltpu.VMEM((3, SLAB, KZ, 128), F32),
+            pltpu.VMEM((SLAB * ROWS, 128), F32),
+            pltpu.VMEM((SLAB * ROWS, 128), F32),
             pltpu.VMEM((96, 128), F32),
             pltpu.VMEM((96, 128), F32),
             pltpu.VMEM((256, 256), BF16),
@@ -669,10 +714,9 @@
             pltpu.VMEM((256, 256), F32),
             pltpu.VMEM((16 * DP, 128), F32),
             pltpu.VMEM((16 * DP, 128), F32),
-            pltpu.VMEM((96, 128), F32),
             pltpu.VMEM((96 * DP, 128), F32),
-            pltpu.VMEM((16, 128), F32),
-            pltpu.VMEM((16 * DP, 128), F32),
+            pltpu.VMEM((8, 128), F32),
+            pltpu.VMEM((8 * DP, 128), F32),
             dma((CH // 2,)),
             dma,
             dma,
@@ -681,6 +725,8 @@
             dma,
             dma((4,)),
             dma((4,)),
+            dma,
+            dma,
             dma,
             dma,
             dma,

time: 78.4 us -> 73.5 us (0.937)
  Pallas kernels: 77.7 us -> 72.7 us
    pallas_call x1, Pallas kernels: 70.2 us -> 65.3 us  [body(): pl.pallas_call(kernel, out_shape=[jax.ShapeDtypeStruct((SLAB * ROWS, 128)...]
where the time goes in v3:
time: 73.5 us; the launch traced here: 73.4 us
  Pallas kernels  72.7 us (99%)
    pallas_call x1, Pallas kernels, body(): pl.pallas_call(kernel, out_shape=[jax.ShapeDtypeStruct((SLAB * ROWS, 128)...  65.3 us
    pallas_call x1, Pallas kernels, body(): pl.pallas_call(last_kernel, out_shape=[block_shape, weight_shape, jax.Sha...  7.48 us

profile of v3, /device:TPU:1, one launch (start us, length us, event | category | flops | bytes accessed | tf_op | source)
XLA Modules:
  0.0 73.4 jit_solution(5893126514320251489)
XLA Ops:
  0.6 65.3 %layer_backward.1 = (f32[512,128]{1,0:T(8,128)}, f32[16,4,128,128]{3,2,1,0:T(8,128)}, f32[2,16,2,384]{3,2,1,0:T(2,128)}) custom-call(f32[16,4,128,128]{3,2,1,0:T(8,128)} %bitcast.3, f32[16,4,128,128]{3,2,1,0:T(8,128)} %bitcast.4, f32[16,16,2,384]{3,2,1,0:T(2,128)} %w_hbm.1, f32[16,16]{1,0:T(8,128)} %pw_hbm.1, bf16[5440,256]{1,0:T(8,128)(2,1)} %constant.4.clone.table_hbm), custom_call_target="tpu_custom_call" | custom-call | tf_op jit(solution)/shard_map/layer_backward/pallas_call | solution.py:689
  65.9 7.5 %input_gradient.1 = (f32[16,4,128,128]{3,2,1,0:T(8,128)}, f32[2,16,2,384]{3,2,1,0:T(2,128)}, f32[16,16]{1,0:T(8,128)}) custom-call(f32[512,128]{1,0:T(8,128)} %get-tuple-element.9.rows_hbm, f32[16,4,128,128]{3,2,1,0:T(8,128)} %get-tuple-element.10.mixed_hbm, f32[2,16,2,384]{3,2,1,0:T(2,128)} %get-tuple-element.11.gs_in, ...), custom_call_target="tpu_custom_call" | custom-call | tf_op jit(solution)/shard_map/input_gradient/pallas_call | solution.py:742

commit v4 on v3

--- a/solution.py
+++ b/solution.py
@@ -176,9 +176,13 @@
             put(4 * t + k, block[SLAB * k : SLAB * k + SLAB])
 
 
-def synthesise_z(block_of, zi_high, zi_low, held, store):
+def synthesise_z(rbuf, zi_high, zi_low, held, store):
+    spare = jnp.zeros((ROWS - KZ, 128), F32)
     for g in range(4):
-        block = block_of(g).T
+        pieces = []
+        for each in range(8):
+            pieces += [rbuf[8 * g + each], spare]
+        block = cat(pieces, 0).T
         high, low = split(cat([block[:64], block[64:]], 1))
         held[pl.ds(64 * g, 64), :] = high
         held[pl.ds(256 + 64 * g, 64), :] = low
@@ -194,7 +198,7 @@
             store[pl.ds(KY + 8 * g + jj, 64, stride=PITCH), :] = out[64 * g : 64 * g + 64, NZ:]
         return carry
 
-    lax.fori_loop(0, 8, step, 0)
+    lax.fori_loop(0, 8, step, 0, unroll=2)
 
 
 def synthesise_y(store, ty_inverse, group):
@@ -225,10 +229,10 @@
 
 def kernel(
     x_hbm, cot_hbm, w_hbm, pw_hbm, table_hbm,
-    last_ref, mixed_hbm, gs_ref,
-    xv, cv, bv, wv, wco, woc, pw, table, store, store2, held, sbuf, rbuf, sbuf3, rbuf3, vv, gv, kron1, kron2, pacc,
-    vsend, vrecv, grecv, psend, precv,
-    xsem, csem, wsem, pwsem, tsem, osem, ssem, rsem, vssem, vrsem, gssem, grsem, hssem, hrsem, pssem, prsem,
+    last_ref, mixed_hbm, gs_ref, gp_ref,
+    xv, cv, bv, wv, wco, woc, pw, table, store, store2, held, sbuf, rbuf, vv, gv, kron1, kron2, pacc,
+    vsend, vrecv, grecv, psend, precv, qsend, qrecv,
+    xsem, csem, wsem, pwsem, tsem, osem, ssem, rsem, vssem, vrsem, gssem, grsem, hssem, hrsem, pssem, prsem, qssem, qrsem,
 ):
     me = lax.axis_index("slab")
     mine = lax.axis_index("dp")
@@ -278,20 +282,10 @@
     zw_high = table.at[pl.ds(ZWH, 480)]
     zw_low = table.at[pl.ds(ZWL, 480)]
 
-    def source(phase, p):
-        if phase == 3:
-            return sbuf3.at[pl.ds(pl.multiple_of(ROWS * p, ROWS), ROWS)]
-        return sbuf.at[phase, p]
-
-    def target(phase, p):
-        if phase == 3:
-            return rbuf3.at[pl.ds(pl.multiple_of(ROWS * p, ROWS), ROWS)]
-        return rbuf.at[phase, p]
-
     def slab_copy(phase, p):
         return pltpu.make_async_remote_copy(
-            src_ref=source(phase, p),
-            dst_ref=target(phase, me),
+            src_ref=sbuf.at[phase, p],
+            dst_ref=rbuf.at[phase, me],
             send_sem=ssem.at[phase],
             recv_sem=rsem.at[phase],
             device_id={"slab": p},
@@ -299,15 +293,10 @@
         )
 
     def slab_all(phase):
-        if phase == 3:
-            every = pl.ds(0, ROWS * (SLAB - 1))
-            src, dst = sbuf3.at[every], rbuf3.at[every]
-        else:
-            every = pl.ds(0, SLAB - 1)
-            src, dst = sbuf.at[phase, every], rbuf.at[phase, every]
+        every = pl.ds(0, SLAB - 1)
         return pltpu.make_async_remote_copy(
-            src_ref=src,
-            dst_ref=dst,
+            src_ref=sbuf.at[phase, every],
+            dst_ref=rbuf.at[phase, every],
             send_sem=ssem.at[phase],
             recv_sem=rsem.at[phase],
             device_id={"slab": lax.rem(me + 1, SLAB)},
@@ -315,11 +304,7 @@
         )
 
     def keep_own(phase):
-        if phase == 3:
-            own = pl.ds(pl.multiple_of(ROWS * me, ROWS), ROWS)
-            rbuf3[own, :] = sbuf3[own, :]
-        else:
-            rbuf[phase, me] = sbuf[phase, me]
+        rbuf[phase, me] = sbuf[phase, me]
 
     def send_one(phase):
         def send(p):
@@ -381,17 +366,7 @@
     for kron, value in ((kron1, wide.T), (kron2, wide)):
         high, low = split(value)
         kron[...] = cat([cat([high, high], 1), cat([low, jnp.zeros_like(low)], 1)], 0)
-    for k in range(KZ + 2, ROWS):
-        sbuf3[pl.ds(k, SLAB, stride=ROWS), :] = jnp.zeros((SLAB, 128), F32)
-
-    def mix_step(yg, carry):
-        y0 = pl.multiple_of(yg * 16, 16)
-        for x in range(XP):
-            high, low = split(rows_of(xv, x, y0))
-            mix_channels(kron1, cat([high, low], 0), bv, x, y0)
-        return carry
-
-    lax.fori_loop(0, NY // 16, mix_step, 0)
+
     w_copy.wait()
 
     def regroup_step(c, carry):
@@ -462,17 +437,18 @@
 
     lax.fori_loop(0, CH, turn_step, 0)
 
+    def mix_step(yg, carry):
+        y0 = pl.multiple_of(yg * 16, 16)
+        for x in range(XP):
+            high, low = split(rows_of(xv, x, y0))
+            mix_channels(kron1, cat([high, low], 0), bv, x, y0)
+        return carry
+
+    lax.fori_loop(0, NY // 16, mix_step, 0)
     c_copy.wait()
     slab_all(1).wait_recv()
 
-    def block_of(g):
-        spare = jnp.zeros((ROWS - KZ, 128), F32)
-        pieces = []
-        for each in range(8):
-            pieces += [rbuf[1, 8 * g + each], spare]
-        return cat(pieces, 0)
-
-    synthesise_z(block_of, zw_high, zw_low, held, store)
+    synthesise_z(rbuf.at[1], zw_high, zw_low, held, store)
 
     def middle_step(o, carry):
         for x in range(XP):
@@ -489,24 +465,20 @@
             analyse_y(cat(grads, 1), ty_stack, store2, x * CH + 2 * o)
         return carry
 
-    lax.fori_loop(0, CH // 2, middle_step, 0)
+    lax.fori_loop(0, CH // 2, middle_step, 0, unroll=2)
     analyse_z(store2, tz_weighted, sbuf, 2, first_group, send_one(2))
 
     pacc[...] = jnp.zeros_like(pacc)
 
-    def back_step(yg, carry):
+    def pointwise_step(yg, carry):
         y0 = pl.multiple_of(yg * 16, 16)
         for x in range(XP):
             high, low = split(rows_of(cv, x, y0))
-            stack = cat([high, low], 0)
-            mix_channels(kron2, stack, bv, x, y0)
             xhigh, xlow = split(rows_of(xv, x, y0))
-            pacc[...] += dot_t(cat([xhigh, xlow], 0), stack)
-        return carry
-
-    lax.fori_loop(0, NY // 16, back_step, 0)
-    o_copy = pltpu.make_async_copy(bv, mixed_hbm, osem)
-    o_copy.start()
+            pacc[...] += dot_t(cat([xhigh, xlow], 0), cat([high, low], 0))
+        return carry
+
+    lax.fori_loop(0, NY // 16, pointwise_step, 0)
     part = pacc[:128, :128] + pacc[:128, 128:] + pacc[128:, :128] + pacc[128:, 128:]
     part = jnp.where(same_row, part, 0.0)
     part = jnp.dot(part, spread, precision=lax.Precision.HIGHEST, preferred_element_type=F32)
@@ -516,29 +488,43 @@
     flat = [cat([part[8 * r + i : 8 * r + i + 1, :] for i in range(8)], 1) for r in range(2)]
     part = cat(flat + [jnp.zeros((6, 128), F32)], 0)
 
-    def p_copy(d):
+    def p_copy(p):
         return pltpu.make_async_remote_copy(
             src_ref=psend,
-            dst_ref=precv.at[pl.ds(pl.multiple_of(8 * mine, 8), 8)],
+            dst_ref=precv.at[pl.ds(pl.multiple_of(8 * me, 8), 8)],
             send_sem=pssem,
             recv_sem=prsem,
-            device_id={"dp": d},
+            device_id={"slab": p},
             device_id_type=MESH,
         )
 
     psend[...] = part
 
     def p_send(d, carry):
-        p_copy(lax.rem(mine + d, DP)).start()
-        return carry
-
-    lax.fori_loop(1, DP, p_send, 0)
-    precv[pl.ds(pl.multiple_of(8 * mine, 8), 8), :] = part
+        p_copy(lax.rem(me + d, SLAB)).start()
+        return carry
+
+    lax.fori_loop(1, SLAB, p_send, 0)
+    precv[pl.ds(pl.multiple_of(8 * me, 8), 8), :] = part
 
     slab_all(2).wait_recv()
     modes = analyse_x(rbuf, 2, rows_high, rows_low)
     gv[:48, :] = modes[:, :128]
     gv[48:, :] = modes[:, 128:]
+
+    def g_copy(d):
+        return pltpu.make_async_remote_copy(
+            src_ref=gv,
+            dst_ref=grecv.at[pl.ds(pl.multiple_of(96 * place, 16), 96)],
+            send_sem=gssem,
+            recv_sem=grsem,
+            device_id={"dp": lax.rem(mine + 2 * d, DP)},
+            device_id_type=MESH,
+        )
+
+    for d in range(1, 4):
+        g_copy(d).start()
+    grecv[pl.ds(pl.multiple_of(96 * place, 16), 96), :] = gv[...]
 
     def back_mode_step(o, carry):
         base = pl.multiple_of(o * 96, 16)
@@ -549,7 +535,7 @@
     back = cat(lax.fori_loop(0, CH, back_mode_step, no_modes), 1)
 
     def put_back(k, value):
-        sbuf3[pl.ds(k, SLAB, stride=ROWS), :] = value
+        sbuf[3, :, k, :] = value
 
     def dp_all(source, target, size, send_sem, recv_sem):
         return pltpu.make_async_remote_copy(
@@ -561,31 +547,42 @@
             device_id_type=MESH,
         )
 
-    p_all = dp_all(precv, precv, 8 * (DP - 1), pssem, prsem)
     v_all = dp_all(vrecv, vrecv, 16 * (DP - 1), vssem, vrsem)
     g_all = dp_all(grecv, grecv, 96 * 3, gssem, grsem)
+    synthesise_x(back, columns_high, columns_low, put_back)
+    send_all(3)
+
+    p_all = pltpu.make_async_remote_copy(
+        src_ref=precv.at[pl.ds(0, 8 * (SLAB - 1))],
+        dst_ref=precv.at[pl.ds(0, 8 * (SLAB - 1))],
+        send_sem=pssem,
+        recv_sem=prsem,
+        device_id={"slab": lax.rem(me + 1, SLAB)},
+        device_id_type=MESH,
+    )
     p_all.wait_recv()
     total = precv[0:8, :]
-    for d in range(1, DP):
-        total = total + precv[8 * d : 8 * d + 8, :]
-    for r in range(2):
-        sbuf3[pl.ds(KZ + r, SLAB, stride=ROWS), :] = jnp.broadcast_to(total[r : r + 1, :], (SLAB, 128))
-    synthesise_x(back, columns_high, columns_low, put_back)
-    send_all(3)
-
-    def g_copy(d):
+    for p in range(1, SLAB):
+        total = total + precv[8 * p : 8 * p + 8, :]
+    qsend[...] = total
+
+    def q_copy(d):
         return pltpu.make_async_remote_copy(
-            src_ref=gv,
-            dst_ref=grecv.at[pl.ds(pl.multiple_of(96 * place, 16), 96)],
-            send_sem=gssem,
-            recv_sem=grsem,
-            device_id={"dp": lax.rem(mine + 2 * d, DP)},
+            src_ref=qsend,
+            dst_ref=qrecv.at[pl.ds(pl.multiple_of(8 * mine, 8), 8)],
+            send_sem=qssem,
+            recv_sem=qrsem,
+            device_id={"dp": d},
             device_id_type=MESH,
         )
 
-    for d in range(1, 4):
-        g_copy(d).start()
-    grecv[pl.ds(pl.multiple_of(96 * place, 16), 96), :] = gv[...]
+    def q_send(d, carry):
+        q_copy(lax.rem(mine + d, DP)).start()
+        return carry
+
+    lax.fori_loop(1, DP, q_send, 0)
+    qrecv[pl.ds(pl.multiple_of(8 * mine, 8), 8), :] = total
+    q_all = dp_all(qrecv, qrecv, 8 * (DP - 1), qssem, qrsem)
     v_all.wait_recv()
     g_all.wait_recv()
     half = pl.ds(pl.multiple_of(core * 384, 16), 384)
@@ -598,8 +595,19 @@
         device_id_type=MESH,
     )
     h_copy.start()
+
+    def back_step(yg, carry):
+        y0 = pl.multiple_of(yg * 16, 16)
+        for x in range(XP):
+            high, low = split(rows_of(cv, x, y0))
+            mix_channels(kron2, cat([high, low], 0), bv, x, y0)
+        return carry
+
+    lax.fori_loop(0, NY // 16, back_step, 0)
+    o_copy = pltpu.make_async_copy(bv, mixed_hbm, osem)
+    o_copy.start()
     slab_all(3).wait_recv()
-    last_ref[...] = rbuf3[...]
+    last_ref[...] = rbuf[3]
     h_copy.wait()
 
     for c in range(2):
@@ -623,13 +631,19 @@
     for phase in range(4):
         slab_all(phase).wait_send()
     p_all.wait_send()
+    q_all.wait_recv()
+    total = qrecv[0:8, :]
+    for d in range(1, DP):
+        total = total + qrecv[8 * d : 8 * d + 8, :]
+    gp_ref[...] = total
+    q_all.wait_send()
     v_all.wait_send()
     g_all.wait_send()
     o_copy.wait()
 
 
 def last_kernel(
-    rows_hbm, mixed_hbm, gs_in, table_hbm, gi_hbm, gs_hbm, gp_hbm,
+    rows_hbm, mixed_hbm, gs_in, gp_in, table_hbm, gi_hbm, gs_hbm, gp_hbm,
     rows_ref, gs_ref, bv, table, held, store, gp, insem, tsem, osem, gssem, gpsem, rsem,
 ):
     rows_copy = pltpu.make_async_copy(rows_hbm, rows_ref, rsem)
@@ -649,14 +663,14 @@
     gs_load.start()
     rows_copy.wait()
     for r in range(2):
-        flat = jnp.sum(rows_ref[pl.ds(KZ + r, SLAB, stride=ROWS), :], axis=0, keepdims=True)
+        flat = gp_in[r : r + 1, :]
         for i in range(8):
             gp[8 * r + i : 8 * r + i + 1, :] = flat[:, CH * i : CH * i + CH] * (1.0 / math.sqrt(DP * NX * NY * NZ))
     gp_copy = pltpu.make_async_copy(gp, gp_hbm, gpsem)
     gp_copy.start()
     table_copy.wait()
     ty_inverse = table.at[pl.ds(0, 128)]
-    synthesise_z(lambda g: rows_ref[pl.ds(128 * g, 128), :], table.at[pl.ds(128, 480)], table.at[pl.ds(608, 480)], held, store)
+    synthesise_z(rows_ref, table.at[pl.ds(128, 480)], table.at[pl.ds(608, 480)], held, store)
 
     def last_step(c, carry):
         in_copy(c).wait()
@@ -686,11 +700,16 @@
     block_shape = jax.ShapeDtypeStruct(block, F32)
     weight_shape = jax.ShapeDtypeStruct((2, CH, 2, KX * KZ), F32)
     store_shape = pltpu.VMEM((CH * XP * PITCH, NZ), F32)
-    rows, mixed, weight_part = pl.pallas_call(
+    rows, mixed, weight_part, point_part = pl.pallas_call(
         kernel,
-        out_shape=[jax.ShapeDtypeStruct((SLAB * ROWS, 128), F32), block_shape, weight_shape],
+        out_shape=[
+            jax.ShapeDtypeStruct((SLAB, KZ, 128), F32),
+            block_shape,
+            weight_shape,
+            jax.ShapeDtypeStruct((8, 128), F32),
+        ],
         in_specs=[hbm] * 5,
-        out_specs=[vmem, hbm, vmem],
+        out_specs=[vmem, hbm, vmem, vmem],
         scratch_shapes=[
             pltpu.VMEM(block, F32),
             pltpu.VMEM(block, F32),
@@ -703,10 +722,8 @@
             store_shape,
             store_shape,
             pltpu.VMEM((512, 256), BF16),
-            pltpu.VMEM((3, SLAB, KZ, 128), F32),
-            pltpu.VMEM((3, SLAB, KZ, 128), F32),
-            pltpu.VMEM((SLAB * ROWS, 128), F32),
-            pltpu.VMEM((SLAB * ROWS, 128), F32),
+            pltpu.VMEM((4, SLAB, KZ, 128), F32),
+            pltpu.VMEM((4, SLAB, KZ, 128), F32),
             pltpu.VMEM((96, 128), F32),
             pltpu.VMEM((96, 128), F32),
             pltpu.VMEM((256, 256), BF16),
@@ -716,6 +733,8 @@
             pltpu.VMEM((16 * DP, 128), F32),
             pltpu.VMEM((96 * DP, 128), F32),
             pltpu.VMEM((8, 128), F32),
+            pltpu.VMEM((8 * SLAB, 128), F32),
+            pltpu.VMEM((8, 128), F32),
             pltpu.VMEM((8 * DP, 128), F32),
             dma((CH // 2,)),
             dma,
@@ -725,6 +744,8 @@
             dma,
             dma((4,)),
             dma((4,)),
+            dma,
+            dma,
             dma,
             dma,
             dma,
@@ -742,10 +763,10 @@
     grad_inputs, grad_spectral, grad_pointwise = pl.pallas_call(
         last_kernel,
         out_shape=[block_shape, weight_shape, jax.ShapeDtypeStruct((CH, CH), F32)],
-        in_specs=[hbm] * 4,
+        in_specs=[hbm, hbm, hbm, vmem, hbm],
         out_specs=[hbm, hbm, hbm],
         scratch_shapes=[
-            pltpu.VMEM((SLAB * ROWS, 128), F32),
+            pltpu.VMEM((SLAB, KZ, 128), F32),
             pltpu.VMEM((2, CH, 2, KX * KZ), F32),
             pltpu.VMEM(block, F32),
             pltpu.VMEM((LAST_TABLE, 256), BF16),
@@ -761,7 +782,7 @@
         ],
         compiler_params=pltpu.CompilerParams(vmem_limit_bytes=60 * 1024 * 1024),
         name="input_gradient",
-    )(rows, mixed, weight_part, last_table)
+    )(rows, mixed, weight_part, point_part, last_table)
     return (grad_inputs[None], grad_spectral, grad_pointwise)
 
 

time: 73.5 us -> 68.3 us (0.929)
  Pallas kernels: 72.7 us -> 67.6 us
    pallas_call x1, Pallas kernels: 65.3 us -> 60.1 us  [body(): pl.pallas_call(kernel, out_shape=[jax.ShapeDtypeStruct((SLAB, KZ, 128), F...]
where the time goes in v4:
time: 68.3 us; the launch traced here: 68.2 us
  Pallas kernels  67.6 us (99%)
    pallas_call x1, Pallas kernels, body(): pl.pallas_call(kernel, out_shape=[jax.ShapeDtypeStruct((SLAB, KZ, 128), F...  60.1 us
    pallas_call x1, Pallas kernels, body(): pl.pallas_call(last_kernel, out_shape=[block_shape, weight_shape, jax.Sha...  7.46 us

profile of v4, /device:TPU:1, one launch (start us, length us, event | category | flops | bytes accessed | tf_op | source)
XLA Modules:
  0.0 68.2 jit_solution(3079182357412669843)
XLA Ops:
  0.6 60.1 %layer_backward.1 = (f32[32,12,128]{2,1,0:T(8,128)}, f32[16,4,128,128]{3,2,1,0:T(8,128)}, f32[2,16,2,384]{3,2,1,0:T(2,128)}, f32[8,128]{1,0:T(8,128)}) custom-call(f32[16,4,128,128]{3,2,1,0:T(8,128)} %bitcast.3, f32[16,4,128,128]{3,2,1,0:T(8,128)} %bitcast.4, f32[16,16,2,384]{3,2,1,0:T(2,128)} %w_hbm.1, f32[16,16]{1,0:T(8,128)} %pw_hbm.1, ...), custom_call_target="tpu_custom_call" | custom-call | tf_op jit(solution)/shard_map/layer_backward/pallas_call | solution.py:703
  60.8 7.5 %input_gradient.1 = (f32[16,4,128,128]{3,2,1,0:T(8,128)}, f32[2,16,2,384]{3,2,1,0:T(2,128)}, f32[16,16]{1,0:T(8,128)}) custom-call(f32[32,12,128]{2,1,0:T(8,128)} %get-tuple-element.10.rows_hbm, f32[16,4,128,128]{3,2,1,0:T(8,128)} %get-tuple-element.11.mixed_hbm, f32[2,16,2,384]{3,2,1,0:T(2,128)} %get-tuple-element.12.gs_in, ...), custom_call_target="tpu_custom_call" | custom-call | tf_op jit(solution)/shard_map/input_gradient/pallas_call | solution.py:763

commit v5 on v4

--- a/solution.py
+++ b/solution.py
@@ -99,6 +99,12 @@
 LAST_TABLE = 128 + 960
 
 
+def each_channel(step, carry):
+    for c in range(CH):
+        carry = step(c, carry)
+    return carry
+
+
 def split(value):
     high = value.astype(BF16)
     low = (value - high.astype(F32)).astype(BF16)
@@ -125,11 +131,10 @@
     store[pl.ds(pl.multiple_of((group + 1) * PITCH, 8), 64), :] = out[:, NZ:]
 
 
-def analyse_z(store, tz_stack, sbuf, phase, first_group, send):
+def analyse_z(store, tz_stack, sbuf, phase, first_group, send, send_own):
     lanes = lax.broadcasted_iota(jnp.int32, (ROWS, 128), 1) < 64
 
-    def step(turn, carry):
-        group = lax.rem(first_group + turn, KY // 4)
+    def analyse(group):
         pieces = []
         for each in range(4):
             j = group * 4 + each
@@ -144,11 +149,18 @@
             second = jnp.where(lanes, pltpu.roll(real, 64, axis=1), imag)
             sbuf[phase, group * 4 + 2 * each] = first[:KZ]
             sbuf[phase, group * 4 + 2 * each + 1] = second[:KZ]
+
+    def step(turn, carry):
+        group = lax.rem(first_group + turn, KY // 4)
+        analyse(group)
         for each in range(4):
             send(group * 4 + each)
         return carry
 
-    lax.fori_loop(0, KY // 4, step, 0)
+    lax.fori_loop(0, 4, step, 0, unroll=4)
+    analyse(lax.rem(first_group + 4, KY // 4))
+    send_own()
+    lax.fori_loop(5, KY // 4, step, 0, unroll=3)
 
 
 def analyse_x(rbuf, phase, rows_high, rows_low):
@@ -198,7 +210,7 @@
             store[pl.ds(KY + 8 * g + jj, 64, stride=PITCH), :] = out[64 * g : 64 * g + 64, NZ:]
         return carry
 
-    lax.fori_loop(0, 8, step, 0, unroll=2)
+    lax.fori_loop(0, 8, step, 0, unroll=8)
 
 
 def synthesise_y(store, ty_inverse, group):
@@ -308,13 +320,15 @@
 
     def send_one(phase):
         def send(p):
-            @pl.when(p != me)
-            def _():
-                slab_copy(phase, p).start()
-
-            @pl.when(p == me)
-            def _():
-                keep_own(phase)
+            slab_copy(phase, p).start()
+
+        return send
+
+    def send_group(phase):
+        def send():
+            for d in range(1, 4):
+                slab_copy(phase, me // 4 * 4 + lax.rem(me + d, 4)).start()
+            keep_own(phase)
 
         return send
 
@@ -355,7 +369,7 @@
 
     lax.fori_loop(0, CH // 2, forward_step, 0)
     pl.semaphore_wait(barrier, SLAB - 1 + DP - 1)
-    analyse_z(store, tz_plain, sbuf, 0, first_group, send_one(0))
+    analyse_z(store, tz_plain, sbuf, 0, first_group, send_one(0), send_group(0))
 
     pw_copy.wait()
     wide = jnp.dot(spread, pw[...], precision=lax.Precision.HIGHEST, preferred_element_type=F32)
@@ -389,13 +403,13 @@
         )
 
     def mode_step(c, carry):
-        base = pl.multiple_of(c * 96, 16)
+        base = c * 96
         wr, wi = wco[pl.ds(base, 48), :], wco[pl.ds(base + 48, 48), :]
         vr, vi = spread_row(vv, c)
         return carry[0] + (wr * vr - wi * vi), carry[1] + (wr * vi + wi * vr)
 
     no_modes = (jnp.zeros((48, 128), F32), jnp.zeros((48, 128), F32))
-    mixed = cat(lax.fori_loop(0, CH, mode_step, no_modes), 1)
+    mixed = cat(each_channel(mode_step, no_modes), 1)
 
     def put_mixed(k, value):
         sbuf[1, :, k, :] = value
@@ -465,8 +479,8 @@
             analyse_y(cat(grads, 1), ty_stack, store2, x * CH + 2 * o)
         return carry
 
-    lax.fori_loop(0, CH // 2, middle_step, 0, unroll=2)
-    analyse_z(store2, tz_weighted, sbuf, 2, first_group, send_one(2))
+    lax.fori_loop(0, CH // 2, middle_step, 0, unroll=4)
+    analyse_z(store2, tz_weighted, sbuf, 2, first_group, send_one(2), send_group(2))
 
     pacc[...] = jnp.zeros_like(pacc)
 
@@ -527,12 +541,12 @@
     grecv[pl.ds(pl.multiple_of(96 * place, 16), 96), :] = gv[...]
 
     def back_mode_step(o, carry):
-        base = pl.multiple_of(o * 96, 16)
+        base = o * 96
         wr, wi = woc[pl.ds(base, 48), :], woc[pl.ds(base + 48, 48), :]
         gr, gi = spread_row(gv, o)
         return carry[0] + (wr * gr + wi * gi), carry[1] + (wr * gi - wi * gr)
 
-    back = cat(lax.fori_loop(0, CH, back_mode_step, no_modes), 1)
+    back = cat(each_channel(back_mode_step, no_modes), 1)
 
     def put_back(k, value):
         sbuf[3, :, k, :] = value

time: 68.3 us -> 67 us (0.981)
  Pallas kernels: 67.6 us -> 66.2 us
    pallas_call x1, Pallas kernels: 60.1 us -> 59.4 us  [body(): pl.pallas_call(kernel, out_shape=[jax.ShapeDtypeStruct((SLAB, KZ, 128), F...]
where the time goes in v5:
time: 67 us; the launch traced here: 66.9 us
  Pallas kernels  66.2 us (99%)
    pallas_call x1, Pallas kernels, body(): pl.pallas_call(kernel, out_shape=[jax.ShapeDtypeStruct((SLAB, KZ, 128), F...  59.4 us
    pallas_call x1, Pallas kernels, body(): pl.pallas_call(last_kernel, out_shape=[block_shape, weight_shape, jax.Sha...  6.88 us

profile of v5, /device:TPU:1, one launch (start us, length us, event | category | flops | bytes accessed | tf_op | source)
XLA Modules:
  0.0 66.9 jit_solution(9762026573945036809)
XLA Ops:
  0.6 59.4 %layer_backward.1 = (f32[32,12,128]{2,1,0:T(8,128)}, f32[16,4,128,128]{3,2,1,0:T(8,128)}, f32[2,16,2,384]{3,2,1,0:T(2,128)}, f32[8,128]{1,0:T(8,128)}) custom-call(f32[16,4,128,128]{3,2,1,0:T(8,128)} %bitcast.3, f32[16,4,128,128]{3,2,1,0:T(8,128)} %bitcast.4, f32[16,16,2,384]{3,2,1,0:T(2,128)} %w_hbm.1, f32[16,16]{1,0:T(8,128)} %pw_hbm.1, ...), custom_call_target="tpu_custom_call" | custom-call | tf_op jit(solution)/shard_map/layer_backward/pallas_call | solution.py:717
  60.0 6.9 %input_gradient.1 = (f32[16,4,128,128]{3,2,1,0:T(8,128)}, f32[2,16,2,384]{3,2,1,0:T(2,128)}, f32[16,16]{1,0:T(8,128)}) custom-call(f32[32,12,128]{2,1,0:T(8,128)} %get-tuple-element.10.rows_hbm, f32[16,4,128,128]{3,2,1,0:T(8,128)} %get-tuple-element.11.mixed_hbm, f32[2,16,2,384]{3,2,1,0:T(2,128)} %get-tuple-element.12.gs_in, ...), custom_call_target="tpu_custom_call" | custom-call | tf_op jit(solution)/shard_map/input_gradient/pallas_call | solution.py:777

commit v6 on v5

--- a/solution.py
+++ b/solution.py
@@ -241,10 +241,10 @@
 
 def kernel(
     x_hbm, cot_hbm, w_hbm, pw_hbm, table_hbm,
-    last_ref, mixed_hbm, gs_ref, gp_ref,
+    rows_hbm, mixed_hbm, gs_hbm, q_hbm,
     xv, cv, bv, wv, wco, woc, pw, table, store, store2, held, sbuf, rbuf, vv, gv, kron1, kron2, pacc,
-    vsend, vrecv, grecv, psend, precv, qsend, qrecv,
-    xsem, csem, wsem, pwsem, tsem, osem, ssem, rsem, vssem, vrsem, gssem, grsem, hssem, hrsem, pssem, prsem, qssem, qrsem,
+    vsend, vrecv, grecv, psend, precv, qsend, gs_ref,
+    xsem, csem, wsem, pwsem, tsem, osem, ssem, rsem, vssem, vrsem, gssem, grsem, hssem, hrsem, pssem, prsem, qssem, qrsem, ownsem, qownsem, gsem,
 ):
     me = lax.axis_index("slab")
     mine = lax.axis_index("dp")
@@ -297,7 +297,7 @@
     def slab_copy(phase, p):
         return pltpu.make_async_remote_copy(
             src_ref=sbuf.at[phase, p],
-            dst_ref=rbuf.at[phase, me],
+            dst_ref=rows_hbm.at[me] if phase == 3 else rbuf.at[phase, me],
             send_sem=ssem.at[phase],
             recv_sem=rsem.at[phase],
             device_id={"slab": p},
@@ -308,15 +308,20 @@
         every = pl.ds(0, SLAB - 1)
         return pltpu.make_async_remote_copy(
             src_ref=sbuf.at[phase, every],
-            dst_ref=rbuf.at[phase, every],
+            dst_ref=rows_hbm.at[every] if phase == 3 else rbuf.at[phase, every],
             send_sem=ssem.at[phase],
             recv_sem=rsem.at[phase],
             device_id={"slab": lax.rem(me + 1, SLAB)},
             device_id_type=MESH,
         )
 
+    own_copy = pltpu.make_async_copy(sbuf.at[3, me], rows_hbm.at[me], ownsem)
+
     def keep_own(phase):
-        rbuf[phase, me] = sbuf[phase, me]
+        if phase == 3:
+            own_copy.start()
+        else:
+            rbuf[phase, me] = sbuf[phase, me]
 
     def send_one(phase):
         def send(p):
@@ -583,7 +588,7 @@
     def q_copy(d):
         return pltpu.make_async_remote_copy(
             src_ref=qsend,
-            dst_ref=qrecv.at[pl.ds(pl.multiple_of(8 * mine, 8), 8)],
+            dst_ref=q_hbm.at[pl.ds(pl.multiple_of(8 * mine, 8), 8)],
             send_sem=qssem,
             recv_sem=qrsem,
             device_id={"dp": d},
@@ -595,8 +600,9 @@
         return carry
 
     lax.fori_loop(1, DP, q_send, 0)
-    qrecv[pl.ds(pl.multiple_of(8 * mine, 8), 8), :] = total
-    q_all = dp_all(qrecv, qrecv, 8 * (DP - 1), qssem, qrsem)
+    q_own = pltpu.make_async_copy(qsend, q_hbm.at[pl.ds(pl.multiple_of(8 * mine, 8), 8)], qownsem)
+    q_own.start()
+    q_all = dp_all(q_hbm, q_hbm, 8 * (DP - 1), qssem, qrsem)
     v_all.wait_recv()
     g_all.wait_recv()
     half = pl.ds(pl.multiple_of(core * 384, 16), 384)
@@ -620,8 +626,6 @@
     lax.fori_loop(0, NY // 16, back_step, 0)
     o_copy = pltpu.make_async_copy(bv, mixed_hbm, osem)
     o_copy.start()
-    slab_all(3).wait_recv()
-    last_ref[...] = rbuf[3]
     h_copy.wait()
 
     for c in range(2):
@@ -642,23 +646,25 @@
             gs_ref[c, :, 0, 128 * t : 128 * t + 128] = total[2 * t]
             gs_ref[c, :, 1, 128 * t : 128 * t + 128] = total[2 * t + 1]
 
+    gs_copy = pltpu.make_async_copy(gs_ref, gs_hbm, gsem)
+    gs_copy.start()
     for phase in range(4):
         slab_all(phase).wait_send()
     p_all.wait_send()
-    q_all.wait_recv()
-    total = qrecv[0:8, :]
-    for d in range(1, DP):
-        total = total + qrecv[8 * d : 8 * d + 8, :]
-    gp_ref[...] = total
     q_all.wait_send()
     v_all.wait_send()
     g_all.wait_send()
     o_copy.wait()
+    own_copy.wait()
+    q_own.wait()
+    gs_copy.wait()
+    slab_all(3).wait_recv()
+    q_all.wait_recv()
 
 
 def last_kernel(
-    rows_hbm, mixed_hbm, gs_in, gp_in, table_hbm, gi_hbm, gs_hbm, gp_hbm,
-    rows_ref, gs_ref, bv, table, held, store, gp, insem, tsem, osem, gssem, gpsem, rsem,
+    rows_hbm, mixed_hbm, gs_in, q_hbm, table_hbm, gi_hbm, gs_hbm, gp_hbm,
+    rows_ref, gs_ref, q_ref, bv, table, held, store, gp, insem, tsem, osem, gssem, gpsem, rsem, qsem,
 ):
     rows_copy = pltpu.make_async_copy(rows_hbm, rows_ref, rsem)
     rows_copy.start()
@@ -675,13 +681,9 @@
         in_copy(c).start()
     gs_load = pltpu.make_async_copy(gs_in, gs_ref, gssem)
     gs_load.start()
+    q_copy = pltpu.make_async_copy(q_hbm, q_ref, qsem)
+    q_copy.start()
     rows_copy.wait()
-    for r in range(2):
-        flat = gp_in[r : r + 1, :]
-        for i in range(8):
-            gp[8 * r + i : 8 * r + i + 1, :] = flat[:, CH * i : CH * i + CH] * (1.0 / math.sqrt(DP * NX * NY * NZ))
-    gp_copy = pltpu.make_async_copy(gp, gp_hbm, gpsem)
-    gp_copy.start()
     table_copy.wait()
     ty_inverse = table.at[pl.ds(0, 128)]
     synthesise_z(rows_ref, table.at[pl.ds(128, 480)], table.at[pl.ds(608, 480)], held, store)
@@ -695,6 +697,16 @@
         out_copy(c).start()
         return carry
 
+    q_copy.wait()
+    total = q_ref[0:8, :]
+    for d in range(1, DP):
+        total = total + q_ref[8 * d : 8 * d + 8, :]
+    total = total * (1.0 / math.sqrt(DP * NX * NY * NZ))
+    for r in range(2):
+        for i in range(8):
+            gp[8 * r + i : 8 * r + i + 1, :] = total[r : r + 1, CH * i : CH * i + CH]
+    gp_copy = pltpu.make_async_copy(gp, gp_hbm, gpsem)
+    gp_copy.start()
     gs_load.wait()
     gs_copy = pltpu.make_async_copy(gs_ref, gs_hbm, gssem)
     gs_copy.start()
@@ -708,7 +720,6 @@
 def body(inputs, cotangent, spectral_weights, pointwise_weights):
     main_table, last_table = (jnp.asarray(table) for table in tables())
     hbm = pl.BlockSpec(memory_space=pltpu.HBM)
-    vmem = pl.BlockSpec(memory_space=pltpu.VMEM)
     block = (CH, XP, NY, NZ)
     dma = pltpu.SemaphoreType.DMA
     block_shape = jax.ShapeDtypeStruct(block, F32)
@@ -720,10 +731,10 @@
             jax.ShapeDtypeStruct((SLAB, KZ, 128), F32),
             block_shape,
             weight_shape,
-            jax.ShapeDtypeStruct((8, 128), F32),
+            jax.ShapeDtypeStruct((8 * DP, 128), F32),
         ],
         in_specs=[hbm] * 5,
-        out_specs=[vmem, hbm, vmem, vmem],
+        out_specs=[hbm] * 4,
         scratch_shapes=[
             pltpu.VMEM(block, F32),
             pltpu.VMEM(block, F32),
@@ -737,7 +748,7 @@
             store_shape,
             pltpu.VMEM((512, 256), BF16),
             pltpu.VMEM((4, SLAB, KZ, 128), F32),
-            pltpu.VMEM((4, SLAB, KZ, 128), F32),
+            pltpu.VMEM((3, SLAB, KZ, 128), F32),
             pltpu.VMEM((96, 128), F32),
             pltpu.VMEM((96, 128), F32),
             pltpu.VMEM((256, 256), BF16),
@@ -749,7 +760,7 @@
             pltpu.VMEM((8, 128), F32),
             pltpu.VMEM((8 * SLAB, 128), F32),
             pltpu.VMEM((8, 128), F32),
-            pltpu.VMEM((8 * DP, 128), F32),
+            pltpu.VMEM((2, CH, 2, KX * KZ), F32),
             dma((CH // 2,)),
             dma,
             dma,
@@ -758,6 +769,9 @@
             dma,
             dma((4,)),
             dma((4,)),
+            dma,
+            dma,
+            dma,
             dma,
             dma,
             dma,
@@ -777,11 +791,12 @@
     grad_inputs, grad_spectral, grad_pointwise = pl.pallas_call(
         last_kernel,
         out_shape=[block_shape, weight_shape, jax.ShapeDtypeStruct((CH, CH), F32)],
-        in_specs=[hbm, hbm, hbm, vmem, hbm],
+        in_specs=[hbm] * 5,
         out_specs=[hbm, hbm, hbm],
         scratch_shapes=[
             pltpu.VMEM((SLAB, KZ, 128), F32),
             pltpu.VMEM((2, CH, 2, KX * KZ), F32),
+            pltpu.VMEM((8 * DP, 128), F32),
             pltpu.VMEM(block, F32),
             pltpu.VMEM((LAST_TABLE, 256), BF16),
             pltpu.VMEM((512, 256), BF16),
@@ -790,6 +805,7 @@
             dma((CH // 2,)),
             dma,
             dma((CH // 2,)),
+            dma,
             dma,
             dma,
             dma,

time: 67 us -> 65.8 us (0.982)
  Pallas kernels: 66.2 us -> 65.1 us
where the time goes in v6:
time: 65.8 us; the launch traced here: 65.7 us
  Pallas kernels  65.1 us (99%)
    pallas_call x1, Pallas kernels, body(): pl.pallas_call(kernel, out_shape=[jax.ShapeDtypeStruct((SLAB, KZ, 128), F...  58.8 us
    pallas_call x1, Pallas kernels, body(): pl.pallas_call(last_kernel, out_shape=[block_shape, weight_shape, jax.Sha...  6.28 us

profile of v6, /device:TPU:1, one launch (start us, length us, event | category | flops | bytes accessed | tf_op | source)
XLA Modules:
  0.0 65.7 jit_solution(7729823940022722895)
XLA Ops:
  0.6 58.8 %layer_backward.1 = (f32[32,12,128]{2,1,0:T(8,128)}, f32[16,4,128,128]{3,2,1,0:T(8,128)}, f32[2,16,2,384]{3,2,1,0:T(2,128)}, f32[64,128]{1,0:T(8,128)}) custom-call(f32[16,4,128,128]{3,2,1,0:T(8,128)} %bitcast.3, f32[16,4,128,128]{3,2,1,0:T(8,128)} %bitcast.4, f32[16,16,2,384]{3,2,1,0:T(2,128)} %w_hbm.1, f32[16,16]{1,0:T(8,128)} %pw_hbm.1, ...), custom_call_target="tpu_custom_call" | custom-call | tf_op jit(solution)/shard_map/layer_backward/pallas_call | solution.py:728
  59.4 6.3 %input_gradient.1 = (f32[16,4,128,128]{3,2,1,0:T(8,128)}, f32[2,16,2,384]{3,2,1,0:T(2,128)}, f32[16,16]{1,0:T(8,128)}) custom-call(f32[32,12,128]{2,1,0:T(8,128)} %get-tuple-element.10.rows_hbm, f32[16,4,128,128]{3,2,1,0:T(8,128)} %get-tuple-element.11.mixed_hbm, f32[2,16,2,384]{3,2,1,0:T(2,128)} %get-tuple-element.12.gs_in, ...), custom_call_target="tpu_custom_call" | custom-call | tf_op jit(solution)/shard_map/input_gradient/pallas_call | solution.py:791

commit v7 on v6

--- a/solution.py
+++ b/solution.py
@@ -569,8 +569,6 @@
     v_all = dp_all(vrecv, vrecv, 16 * (DP - 1), vssem, vrsem)
     g_all = dp_all(grecv, grecv, 96 * 3, gssem, grsem)
     synthesise_x(back, columns_high, columns_low, put_back)
-    send_all(3)
-
     p_all = pltpu.make_async_remote_copy(
         src_ref=precv.at[pl.ds(0, 8 * (SLAB - 1))],
         dst_ref=precv.at[pl.ds(0, 8 * (SLAB - 1))],
@@ -603,6 +601,8 @@
     q_own = pltpu.make_async_copy(qsend, q_hbm.at[pl.ds(pl.multiple_of(8 * mine, 8), 8)], qownsem)
     q_own.start()
     q_all = dp_all(q_hbm, q_hbm, 8 * (DP - 1), qssem, qrsem)
+    send_all(3)
+
     v_all.wait_recv()
     g_all.wait_recv()
     half = pl.ds(pl.multiple_of(core * 384, 16), 384)

time: 65.8 us -> 67.4 us (1.024)
  the two profiles are of different devices: /device:TPU:1 before, /device:TPU:32 now
where the time goes in v7:
time: 67.4 us; the launch traced here: 67.3 us
  Pallas kernels  66.7 us (99%)
    pallas_call x1, Pallas kernels, body(): pl.pallas_call(kernel, out_shape=[jax.ShapeDtypeStruct((SLAB, KZ, 128), F...  60.4 us
    pallas_call x1, Pallas kernels, body(): pl.pallas_call(last_kernel, out_shape=[block_shape, weight_shape, jax.Sha...  6.29 us

profile of v7, /device:TPU:32, one launch (start us, length us, event | category | flops | bytes accessed | tf_op | source)
XLA Modules:
  0.0 67.3 jit_solution(1337398673401211831)
XLA Ops:
  0.6 60.4 %layer_backward.1 = (f32[32,12,128]{2,1,0:T(8,128)}, f32[16,4,128,128]{3,2,1,0:T(8,128)}, f32[2,16,2,384]{3,2,1,0:T(2,128)}, f32[64,128]{1,0:T(8,128)}) custom-call(f32[16,4,128,128]{3,2,1,0:T(8,128)} %bitcast.3, f32[16,4,128,128]{3,2,1,0:T(8,128)} %bitcast.4, f32[16,16,2,384]{3,2,1,0:T(2,128)} %w_hbm.1, f32[16,16]{1,0:T(8,128)} %pw_hbm.1, ...), custom_call_target="tpu_custom_call" | custom-call | tf_op jit(solution)/shard_map/layer_backward/pallas_call | solution.py:728
  61.0 6.3 %input_gradient.1 = (f32[16,4,128,128]{3,2,1,0:T(8,128)}, f32[2,16,2,384]{3,2,1,0:T(2,128)}, f32[16,16]{1,0:T(8,128)}) custom-call(f32[32,12,128]{2,1,0:T(8,128)} %get-tuple-element.10.rows_hbm, f32[16,4,128,128]{3,2,1,0:T(8,128)} %get-tuple-element.11.mixed_hbm, f32[2,16,2,384]{3,2,1,0:T(2,128)} %get-tuple-element.12.gs_in, ...), custom_call_target="tpu_custom_call" | custom-call | tf_op jit(solution)/shard_map/input_gradient/pallas_call | solution.py:791
